TPU v7x, 32 devices: a whole 2x2x4 slice. The times are simulated.
32 devices in a mesh: dp: 4 (over y, x), ctx: 8 (over z, core).
Axes of the slice: x: 2, y: 2, z: 4, core: 2. Of those that a mesh axis runs over, the one named last changes fastest.
Arguments:
- gate_in: bfloat16 [4, 1024, 2048], P('dp', 'ctx'), may hold values from -6 to 6
- key_in: bfloat16 [4, 1024, 2048], P('dp', 'ctx'), may hold values from -6 to 6
- value_in: bfloat16 [4, 1024, 2048], P('dp', 'ctx'), may hold values from -6 to 6
- cotangent: bfloat16 [4, 1024, 2048], P('dp', 'ctx'), may hold values from -6 to 6
- doc_starts: int32 [4, 3], P('dp'), may hold values from 0 to 768, as said below
- filters: bfloat16 [128, 128], replicated, may hold values from -0.5 to 0.5
Outputs:
- output: bfloat16 [4, 1024, 2048], P('dp', 'ctx')
- grad_query: bfloat16 [4, 1024, 2048], P('dp', 'ctx')
- grad_key: bfloat16 [4, 1024, 2048], P('dp', 'ctx')
- grad_value: bfloat16 [4, 1024, 2048], P('dp', 'ctx')
- filter_grad: float32 [128, 128], replicated
Inputs may be any that keep to these rules, and one draw needn't show every extreme that they name: `doc_starts`: each row holds 3 strictly rising multiples of 128; the first is 0 and the last is 768.
All inputs are finite; a program needn't handle non-finite values.
Results may differ from a plain program's by a relative error of at most 0.0049.
Values may be sent and summed in bfloat16 or wider, within the bound.
No kernel may reach another device: no remote copies, remote signals or barrier semaphores. Data moves between devices by JAX's collectives and lax.ppermute only.
A program may use at most 192 MiB of HBM per device.

v0:
```python
import functools

import jax
import jax.numpy as jnp
from jax import lax
from jax.experimental import pallas as pl
from jax.experimental.pallas import tpu as pltpu
from jax.sharding import PartitionSpec as P

LANES = 128
ROW_BLOCK = 32
MIB = 1024 * 1024
CHUNKS = 4
PIECES = 2
CHUNK = 512
FIRST_VMEM = 213 * MIB // 4
GATES_VMEM = 101 * MIB // 2
VMEM = pl.BlockSpec(memory_space=pltpu.VMEM)
SMEM = pl.BlockSpec(memory_space=pltpu.SMEM)


def iota(shape, dim):
    return lax.broadcasted_iota(jnp.int32, shape, dim)


def exchange(array, first):
    seqs, blocks = lax.axis_size("dp"), lax.axis_size("ctx")
    pairs = []
    for seq in range(seqs):
        for block in range(blocks):
            to_seq, to_block = seq, (block - first ^ 1) + first
            if not 0 <= to_block < blocks:
                to_seq, to_block = seq ^ 1, block
            pairs.append((seq * blocks + block, to_seq * blocks + to_block))
    return lax.ppermute(array, ("dp", "ctx"), pairs)


def swapped(array, axis, step):
    size = lax.axis_size(axis)
    return lax.ppermute(array, axis, [(i, i ^ step) for i in range(size)])


def swapped(array, axis, step):
    size = lax.axis_size(axis)
    return lax.ppermute(array, axis, [(i, i ^ step) for i in range(size)])


def along(array, axis):
    size = lax.axis_size(axis)
    pairs = [(i, i + 2 if i % 2 else i - 2) for i in range(size)]
    return lax.ppermute(array, axis, [(i, j) for i, j in pairs if 0 <= j < size])


def add_kernel(*refs):
    *terms, _, out_ref = [ref for ref in refs]
    terms = [term[...] for term in terms]
    while len(terms) > 1:
        terms = [sum(terms[i + 1 : i + 2], terms[i]) for i in range(0, len(terms), 2)]
    out_ref[...] = terms[0]


def add(terms, after):
    return pl.pallas_call(
        add_kernel,
        in_specs=[VMEM] * len(terms) + [pl.BlockSpec(memory_space=pl.ANY)],
        out_specs=VMEM,
        out_shape=jax.ShapeDtypeStruct(terms[0].shape, terms[0].dtype),
        name="add",
        compiler_params=pltpu.CompilerParams(vmem_limit_bytes=MIB),
    )(*terms, after)


def sum_devices(mine, beside):
    turn = 0
    for axis, step in (("dp", 1), ("ctx", 2)):
        size = lax.axis_size(axis)
        while step < size:
            count = 4 if axis == "dp" and 4 * step <= size else 2
            others = [swapped(mine, axis, step * i) for i in range(1, count)]
            mine = add([mine] + others, beside(mine, turn))
            step, turn = count * step, turn + 1
    return mine


def join_kernel(mine_ref, other_ref, out_ref):
    count = mine_ref.shape[0]
    odd = lax.axis_index("ctx") % 2
    out_ref[pl.ds(pl.multiple_of(odd * count, count), count)] = mine_ref[...]
    out_ref[pl.ds(pl.multiple_of((1 - odd) * count, count), count)] = other_ref[...]


def join(mine, other):
    count, taps = mine.shape
    return pl.pallas_call(
        join_kernel,
        in_specs=[VMEM] * 2,
        out_specs=VMEM,
        out_shape=jax.ShapeDtypeStruct((2 * count, taps), mine.dtype),
        name="join",
        compiler_params=pltpu.CompilerParams(vmem_limit_bytes=MIB),
    )(mine, other)


def reversal(taps):
    flip = iota((taps, taps), 0) + iota((taps, taps), 1) == taps - 1
    return jnp.where(flip, 1.0, 0.0).astype(jnp.bfloat16)


def flipped(reverse, array):
    return jnp.dot(reverse, array, preferred_element_type=jnp.float32)


def masked(array, keep):
    return array * jnp.concatenate([keep] * (array.shape[0] // keep.shape[0]), axis=0)


def bf16_product(one, two):
    return (one.astype(jnp.float32) * two.astype(jnp.float32)).astype(jnp.bfloat16)


def first_kernel(q_hbm, k_hbm, v_hbm, ct_hbm, other_ref, held, sems):
    taps, half = other_ref.shape
    block = half // CHUNKS
    odd = lax.axis_index("ctx") % 2 == 1
    reverse = reversal(taps)

    def make(sources, start, finish):
        copies = []
        for c in range(CHUNKS):
            for a, source in enumerate(sources):
                copy = pltpu.make_async_copy(
                    source.at[:, pl.ds(start + c * block, block)],
                    held.at[a, :, pl.ds(c * block, block)],
                    sems.at[c, a],
                )
                copy.start()
                copies.append(copy)
        for copy in copies:
            copy.wait()
        other_ref[...] = finish(bf16_product(held[0], held[1]))

    @pl.when(odd)
    def _():
        make((k_hbm, v_hbm), 0, lambda u: u)

    @pl.when(jnp.logical_not(odd))
    def _():
        make((ct_hbm, q_hbm), half, lambda dy: flipped(reverse, dy).astype(jnp.bfloat16))


def first_gate(q, k, v, ct):
    taps, channels = q.shape
    half = channels // 2
    return pl.pallas_call(
        first_kernel,
        in_specs=[pl.BlockSpec(memory_space=pltpu.HBM)] * 4,
        out_specs=VMEM,
        out_shape=jax.ShapeDtypeStruct((taps, half), jnp.bfloat16),
        scratch_shapes=[
            pltpu.VMEM((2, taps, half), jnp.bfloat16),
            pltpu.SemaphoreType.DMA((CHUNKS, 2)),
        ],
        name="first_gate",
        cost_estimate=pl.CostEstimate(
            flops=taps * taps * channels, bytes_accessed=3 * taps * channels, transcendentals=0
        ),
        compiler_params=pltpu.CompilerParams(vmem_limit_bytes=FIRST_VMEM),
    )(q, k, v, ct)


def gates_kernel(
    after_ref, q_hbm, k_hbm, v_hbm, ct_hbm,
    q_ref, k_ref, v_ref, ct_ref, near_own_ref, near_other_ref, own_ref, sems,
):
    del after_ref
    taps, channels = q_ref.shape
    half = channels // 2
    block = channels // CHUNKS
    pairs = ((k_hbm, k_ref), (v_hbm, v_ref), (q_hbm, q_ref), (ct_hbm, ct_ref))
    copies = []
    for c in range(CHUNKS):
        cols = pl.ds(c * block, block)
        for a, (source, target) in enumerate(pairs):
            copy = pltpu.make_async_copy(source.at[:, cols], target.at[:, cols], sems.at[c, a])
            copy.start()
            copies.append(copy)
    odd = lax.axis_index("ctx") % 2 == 1
    reverse = reversal(taps)
    for c in range(CHUNKS):
        cols = pl.ds(c * block, block)
        sent = pl.ds(c * block % half, block)
        for copy in copies[4 * c : 4 * c + 4]:
            copy.wait()

        def make_u():
            return bf16_product(k_ref[:, cols], v_ref[:, cols])

        def make_dy():
            dy = bf16_product(ct_ref[:, cols], q_ref[:, cols])
            return flipped(reverse, dy).astype(jnp.bfloat16)

        @pl.when(odd)
        def _():
            near_ref = near_own_ref if c * block >= half else near_other_ref
            near_ref[:, sent] = make_dy()
            if c * block >= half:
                own_ref[:, sent] = make_u()

        @pl.when(jnp.logical_not(odd))
        def _():
            near_ref = near_own_ref if c * block < half else near_other_ref
            near_ref[:, sent] = make_u()
            if c * block < half:
                own_ref[:, sent] = make_dy()


def gates(after, q, k, v, ct):
    taps, channels = q.shape

    def shape(*dims):
        return jax.ShapeDtypeStruct(dims, jnp.bfloat16)

    half = channels // 2
    return pl.pallas_call(
        gates_kernel,
        in_specs=[pl.BlockSpec(memory_space=pl.ANY)]
        + [pl.BlockSpec(memory_space=pltpu.HBM)] * 4,
        out_specs=[VMEM] * 7,
        out_shape=[shape(taps, channels)] * 4 + [shape(taps, half)] * 3,
        scratch_shapes=[pltpu.SemaphoreType.DMA((CHUNKS, 4))],
        name="gates",
        cost_estimate=pl.CostEstimate(
            flops=2 * taps * taps * channels, bytes_accessed=12 * taps * channels, transcendentals=0
        ),
        compiler_params=pltpu.CompilerParams(vmem_limit_bytes=GATES_VMEM),
    )(after, q, k, v, ct)


def masks_kernel(taps, starts_ref, after_ref, keep_ref):
    del after_ref
    here = lax.axis_index("ctx")
    for side in range(2):
        found = (here + side) % lax.axis_size("ctx") == 0
        for d in range(starts_ref.shape[0]):
            found = jnp.logical_or(found, starts_ref[d] == (here + side) * taps)
        keep = jnp.where(found, 0.0, 1.0)
        keep_ref[side] = jnp.full(keep_ref.shape[1:], keep).astype(jnp.bfloat16)


def masks(starts, after):
    return pl.pallas_call(
        functools.partial(masks_kernel, after.shape[0]),
        in_specs=[SMEM, pl.BlockSpec(memory_space=pl.ANY)],
        out_specs=VMEM,
        out_shape=jax.ShapeDtypeStruct((2, 16, LANES), jnp.bfloat16),
        name="masks",
        compiler_params=pltpu.CompilerParams(vmem_limit_bytes=MIB),
    )(starts, after)


def toeplitz_kernel(filters_ref, after_ref, out_ref, done_ref):
    del after_ref
    count, taps = filters_ref.shape
    lines = filters_ref[...].astype(jnp.float32)
    current = iota((taps, taps), 0) <= iota((taps, taps), 1)
    for f in range(count):
        tile = jnp.broadcast_to(lines[f : f + 1], (taps, taps))
        tile = pltpu.roll(tile, 0, 1, stride=1, stride_axis=0)
        out_ref[f, :taps] = jnp.where(current, 0.0, tile).astype(jnp.bfloat16)
        out_ref[f, taps:] = jnp.where(current, tile, 0.0).astype(jnp.bfloat16)
    done_ref[...] = jnp.zeros_like(done_ref)


def toeplitz(filters, after):
    count, taps = filters.shape
    return pl.pallas_call(
        toeplitz_kernel,
        in_specs=[VMEM, pl.BlockSpec(memory_space=pl.ANY)],
        out_specs=[VMEM] * 2,
        out_shape=[
            jax.ShapeDtypeStruct((count, 2 * taps, taps), jnp.bfloat16),
            jax.ShapeDtypeStruct((8, LANES), jnp.float32),
        ],
        name="toeplitz",
        cost_estimate=pl.CostEstimate(
            flops=count * taps * taps * 64, bytes_accessed=4 * count * taps * taps, transcendentals=0
        ),
        compiler_params=pltpu.CompilerParams(vmem_limit_bytes=8 * MIB),
    )(filters, after)


def filter_grad_kernel(
    width, near_ref, own_ref, keep_ref, near_in_ref, extra_ref, far_in_ref, after_ref, out_ref, lines
):
    del after_ref
    taps, half = far_in_ref.shape
    per_group = LANES // width
    odd = lax.axis_index("ctx") % 2
    keep_far = keep_ref[odd]
    keep_near = keep_ref[1 - odd]
    lane_filter = iota((ROW_BLOCK, LANES), 1) // width
    fold = iota((ROW_BLOCK, taps), 1) + iota((ROW_BLOCK, taps), 0) < ROW_BLOCK
    for group in range(half // LANES):
        at = group * LANES
        cols = pl.ds(at, LANES)
        near = near_ref[:, cols]
        pairs = (
            (own_ref[:, cols], masked(far_in_ref[:, cols], keep_far), near),
            (near_in_ref[:, cols], masked(near, keep_near), extra_ref[:, cols]),
        )
        left, right = [], []
        for moving, beyond, fixed in pairs:
            window = jnp.concatenate([beyond, fixed], axis=0)
            for start in range(0, taps, ROW_BLOCK):
                piece = moving[start : start + ROW_BLOCK]
                left.append(
                    jnp.concatenate(
                        [jnp.where(lane_filter == i, piece, 0) for i in range(per_group)], axis=0
                    )
                )
                right.append(window[taps - ROW_BLOCK - start : 2 * taps - start])
        product = lax.dot_general(
            jnp.concatenate(left, axis=1),
            jnp.concatenate(right, axis=1),
            (((1,), (1,)), ((), ())),
            preferred_element_type=jnp.float32,
        )
        rows = []
        for i in range(per_group):
            tile = product[i * ROW_BLOCK : (i + 1) * ROW_BLOCK]
            high = jnp.concatenate(
                [tile[:, taps:], jnp.zeros((ROW_BLOCK, taps - ROW_BLOCK), jnp.float32)], axis=1
            )
            tile = jnp.where(fold, high, tile[:, :taps])
            tile = pltpu.roll(tile, taps - ROW_BLOCK + 1, 1, stride=1, stride_axis=0)
            rows.append(jnp.sum(tile, axis=0, keepdims=True))
        lines[group * per_group : (group + 1) * per_group] = jnp.concatenate(rows, axis=0)
    flip = jnp.where((iota((taps, taps), 0) + iota((taps, taps), 1)) % taps == 0, 1.0, 0.0)
    out_ref[...] = jnp.dot(
        lines[...], flip, preferred_element_type=jnp.float32, precision=lax.Precision.HIGHEST
    )


def filter_gradient(near, own, keep, near_in, extra, far_in, after, width):
    taps, half = own.shape
    count = half // width
    return pl.pallas_call(
        functools.partial(filter_grad_kernel, width),
        in_specs=[VMEM] * 6 + [pl.BlockSpec(memory_space=pl.ANY)],
        out_specs=VMEM,
        out_shape=jax.ShapeDtypeStruct((count, taps), jnp.float32),
        scratch_shapes=[pltpu.VMEM((count, taps), jnp.float32)],
        name="filter_gradient",
        cost_estimate=pl.CostEstimate(
            flops=4 * count * taps * taps * 256, bytes_accessed=16 * taps * half, transcendentals=0
        ),
        compiler_params=pltpu.CompilerParams(vmem_limit_bytes=8 * MIB),
    )(near, own, keep, near_in, extra, far_in, after)


def outputs_kernel(
    width, base, q_ref, k_ref, v_ref, ct_ref, tiles_ref, near_ref, far_ref, keep_ref,
    near_in_ref, far_in_ref, *rest,
):
    *results, sems = rest[-5:]
    *targets, done_ref = rest[-10:-5]
    out, grad_q, grad_k, grad_v = results
    taps, half = far_ref.shape
    channels = out.shape[1]
    per_group = LANES // width
    odd = lax.axis_index("ctx") % 2
    keep_far = keep_ref[odd]
    keep_near = keep_ref[1 - odd]
    second = odd if base < half else 1 - odd
    base = base % half
    first = pl.multiple_of(second * half, half)
    reverse = reversal(taps)
    copies = []

    def send(which, at, sem):
        own = pl.ds(at, CHUNK)
        cols = pl.ds(pl.multiple_of(first + base + at, CHUNK), CHUNK)
        copy = pltpu.make_async_copy(results[which].at[:, own], targets[which].at[:, cols], sem)
        copy.start()
        copies.append(copy)

    lines = []
    for lane in range(0, channels, LANES):
        sent = pl.ds(base + lane, LANES)
        near_lines = jnp.concatenate(
            [masked(far_in_ref[:, sent], keep_far).T, near_ref[:, sent].T], axis=1
        )
        far_lines = jnp.concatenate(
            [masked(near_in_ref[:, sent], keep_near).T, far_ref[:, sent].T], axis=1
        )
        lines.append((lane, near_lines, far_lines))
    sums = []
    for lane, near_lines, far_lines in lines:
        at = (first + base + lane) // width
        near_parts, far_parts = [], []
        for i in range(per_group):
            rows = slice(i * width, (i + 1) * width)
            both = jnp.concatenate([near_lines[rows], far_lines[rows]], axis=0)
            part = jnp.dot(both, tiles_ref[at + i], preferred_element_type=jnp.float32)
            near_parts.append(part[:width])
            far_parts.append(part[width:])
        near_sum = jnp.concatenate(near_parts, axis=0)
        far_sum = jnp.concatenate(far_parts, axis=0)
        y = jnp.where(odd == 1, far_sum, near_sum).T
        mixed = jnp.where(odd == 1, near_sum, far_sum).T
        sums.append((lane, y, mixed))
    for chunk in range(0, channels, CHUNK):
        whole = pl.ds(pl.multiple_of(first + base + chunk, CHUNK), CHUNK)
        k_turned = flipped(reverse, k_ref[:, whole])
        v_turned = flipped(reverse, v_ref[:, whole])
        k_parts, v_parts = [], []
        for lane, y, mixed in sums[chunk // LANES : (chunk + CHUNK) // LANES]:
            own = pl.ds(lane, LANES)
            cols = pl.ds(pl.multiple_of(first + base + lane, LANES), LANES)
            out[:, own] = (q_ref[:, cols].astype(jnp.float32) * y).astype(jnp.bfloat16)
            grad_q[:, own] = (ct_ref[:, cols].astype(jnp.float32) * y).astype(jnp.bfloat16)
            lanes = slice(lane - chunk, lane - chunk + LANES)
            k_parts.append((mixed * v_turned[:, lanes]).astype(jnp.bfloat16))
            v_parts.append((mixed * k_turned[:, lanes]).astype(jnp.bfloat16))
        own = pl.ds(chunk, CHUNK)
        turn = chunk // CHUNK
        send(0, chunk, sems.at[turn, 0])
        send(1, chunk, sems.at[turn, 1])
        grad_k[:, own] = flipped(reverse, jnp.concatenate(k_parts, axis=1)).astype(jnp.bfloat16)
        send(2, chunk, sems.at[turn, 2])
        grad_v[:, own] = flipped(reverse, jnp.concatenate(v_parts, axis=1)).astype(jnp.bfloat16)
        send(3, chunk, sems.at[turn, 3])
    for copy in copies:
        copy.wait()
    done_ref[...] = jnp.zeros_like(done_ref)


def outputs(piece, operands, results, after, width):
    taps, channels = operands[0].shape
    part = channels // PIECES
    anywhere = pl.BlockSpec(memory_space=pl.ANY)
    shape = jax.ShapeDtypeStruct((taps, channels), jnp.bfloat16)
    *results, done = pl.pallas_call(
        functools.partial(outputs_kernel, width, piece * part),
        in_specs=[VMEM] * len(operands) + [anywhere] * (1 + len(results)),
        out_specs=[anywhere] * 4 + [VMEM],
        out_shape=[shape] * 4 + [jax.ShapeDtypeStruct((8, LANES), jnp.float32)],
        input_output_aliases={len(operands) + 1 + i: i for i in range(len(results))},
        scratch_shapes=[pltpu.VMEM((taps, part), jnp.bfloat16)] * 4
        + [pltpu.SemaphoreType.DMA((part // CHUNK, 4))],
        name=f"outputs_{piece}",
        cost_estimate=pl.CostEstimate(
            flops=16 * (part // width) * taps * taps * 256,
            bytes_accessed=24 * taps * part,
            transcendentals=0,
        ),
        compiler_params=pltpu.CompilerParams(vmem_limit_bytes=8 * MIB),
    )(*operands, after, *results)
    return results, done


def per_device(gate_in, key_in, value_in, cotangent, doc_starts, filters):
    taps = filters.shape[1]
    width = gate_in.shape[2] // filters.shape[0]
    assert gate_in.shape[1] == taps
    q, k, v, ct = gate_in[0], key_in[0], value_in[0], cotangent[0]
    other = first_gate(q, k, v, ct)
    other_in = exchange(other, 1)
    q, k, v, ct, near_own, near_other, own = gates(other, q, k, v, ct)
    near_in_own = exchange(near_other, 0)
    extra = exchange(other, 0)
    own_in = exchange(own, 1)
    near_in_other = exchange(near_own, 0)
    keep = masks(doc_starts[0], near_other)
    mine = filter_gradient(near_own, own, keep, near_in_own, extra, other_in, near_in_other, width)
    halves = (
        (near_own, own, keep, near_in_own, other_in),
        (near_other, other, keep, near_in_other, own_in),
    )
    tiles = None
    results = []

    def beside(after, turn):
        nonlocal tiles, results
        if turn == 0:
            tiles, after = toeplitz(filters, after)
        elif turn <= PIECES:
            operands = (q, k, v, ct, tiles, *halves[turn - 1])
            results, after = outputs(turn - 1, operands, results, after, width)
        return after

    mine = sum_devices(mine, beside)
    filter_grad = join(mine, exchange(mine, 0))
    return tuple(array[None] for array in results) + (filter_grad,)


def solution(mesh):
    split = P("dp", "ctx", None)
    return jax.shard_map(
        per_device,
        mesh=mesh,
        in_specs=(split, split, split, split, P("dp", None), P()),
        out_specs=(split, split, split, split, P()),
        check_vma=False,
    )
```

profile of v0, /device:TPU:0, one launch (start us, length us, event | category | flops | bytes accessed | tf_op | source)
XLA Modules:
  0.0 29.1 jit_solution(14120311629653148865)
XLA Ops:
  0.6 1.4 %first_gate.1.after_ref.far_ref = bf16[128,1024]{1,0:T(8,128)(2,1)S(1)} custom-call(bf16[128,2048]{1,0:T(8,128)(2,1)} %bitcast.10, bf16[128,2048]{1,0:T(8,128)(2,1)} %bitcast.12, bf16[128,2048]{1,0:T(8,128)(2,1)} %bitcast.14, bf16[128,2048]{1,0:T(8,128)(2,1)} %bitcast.16), custom_call_target="tpu_custom_call" | custom-call | flops 33554432 | bytes 786432 | tf_op jit(solution)/shard_map/first_gate/pallas_call | solution.py:154
  2.0 3.0 %collective-permute-start.2 = (bf16[128,1024]{1,0:T(8,128)(2,1)S(1)}, bf16[128,1024]{1,0:T(8,128)(2,1)S(1)}, u32[]{:S(2)}, u32[]{:S(2)}) collective-permute-start(bf16[128,1024]{1,0:T(8,128)(2,1)S(1)} %first_gate.1.after_ref.far_ref), channel_id=1, source_target_pairs={{0,8},{1,2},{2,1},{3,4},{4,3},{5,6},{6,5},{7,15},{8,0},{9,10},{10,... | collective-permute-start | bytes 786440 | tf_op jit(solution)/shard_map/ppermute | solution.py:35
  5.0 0.2 collective-permute-start.1
  5.2 1.8 %gates.1 = (bf16[128,2048]{1,0:T(8,128)(2,1)S(1)}, bf16[128,2048]{1,0:T(8,128)(2,1)S(1)}, bf16[128,2048]{1,0:T(8,128)(2,1)S(1)}, bf16[128,2048]{1,0:T(8,128)(2,1...) custom-call(bf16[128,1024]{1,0:T(8,128)(2,1)S(1)} %first_gate.1.after_ref.far_ref, ...), custom_call_target="tpu_custom_call" | custom-call | flops 67108864 | bytes 3145728 | tf_op jit(solution)/shard_map/gates/pallas_call | solution.py:224
  7.1 0.6 %collective-permute-start.3 = (bf16[128,1024]{1,0:T(8,128)(2,1)S(1)}, bf16[128,1024]{1,0:T(8,128)(2,1)S(1)}, u32[]{:S(2)}, u32[]{:S(2)}) collective-permute-start(bf16[128,1024]{1,0:T(8,128)(2,1)S(1)} %get-tuple-element.28.near_ref), channel_id=1, source_target_pairs={{0,1},{1,0},{2,3},{3,2},{4,5},{5,4},{6,7},{7,6},{8,9},{9,8},{10,11... | collective-permute-start | bytes 786440 | tf_op jit(solution)/shard_map/ppermute | solution.py:35
  7.7 0.1 collective-permute-start
  7.7 0.7 %copy-done = s32[1,3]{1,0:T(1,128)S(1)} copy-done((s32[1,3]{1,0:T(1,128)S(1)}, s32[1,3]{1,0:T(1,128)}, u32[]{:S(2)}) %copy-start) | copy-done | bytes 36
  8.4 0.6 %masks.1.keep_ref = bf16[2,16,128]{2,1,0:T(8,128)(2,1)S(1)} custom-call(s32[3]{0:T(128)S(1)} %bitcast.9, bf16[128,1024]{1,0:T(8,128)(2,1)S(1)} %get-tuple-element.30.after_ref.near_ref), custom_call_target="tpu_custom_call" | custom-call | tf_op jit(solution)/shard_map/masks/pallas_call | solution.py:251
  9.0 0.4 %collective-permute-done.2.far_in_ref = bf16[128,1024]{1,0:T(8,128)(2,1)S(1)} collective-permute-done((bf16[128,1024]{1,0:T(8,128)(2,1)S(1)}, bf16[128,1024]{1,0:T(8,128)(2,1)S(1)}, u32[]{:S(2)}, u32[]{:S(2)}) %collective-permute-start.2) | collective-permute-done | bytes 262176 | tf_op jit(solution)/shard_map/ppermute | solution.py:35
  9.4 1.6 %filter_gradient.1.after_ref.refs_0_ = f32[64,128]{1,0:T(8,128)S(1)} custom-call(bf16[128,1024]{1,0:T(8,128)(2,1)S(1)} %get-tuple-element.28.near_ref, bf16[128,1024]{1,0:T(8,128)(2,1)S(1)} %get-tuple-element.29.own_ref.far_ref, bf16[2,16,128]{2,1,0:T(8,128)(2,1)S(1)} %masks.1.keep_ref, bf16[128,1024]{1,0:T(8,128)(2,1)S(1)} %collective-permute-done.near_in_ref, ...), custom_call_target="tpu_custom_call" | custom-call | flops 1073741824 | bytes 2097152 | tf_op jit(solution)/shard_map/filter_gradient/pallas_call | solution.py:347
  11.0 3.0 %collective-permute-start.7 = (f32[64,128]{1,0:T(8,128)S(1)}, f32[64,128]{1,0:T(8,128)S(1)}, u32[]{:S(2)}, u32[]{:S(2)}) collective-permute-start(f32[64,128]{1,0:T(8,128)S(1)} %filter_gradient.1.after_ref.refs_0_), channel_id=1, source_target_pairs={{0,24},{8,16},{16,8},{24,0},{1,25},{9,17},{17,9},{25,1},{2,26},{10... | collective-permute-start | bytes 98312 | tf_op jit(solution)/shard_map/ppermute | solution.py:45
  14.0 0.5 %collective-permute-start.6 = (f32[64,128]{1,0:T(8,128)S(1)}, f32[64,128]{1,0:T(8,128)S(1)}, u32[]{:S(2)}, u32[]{:S(2)}) collective-permute-start(f32[64,128]{1,0:T(8,128)S(1)} %filter_gradient.1.after_ref.refs_0_), channel_id=1, source_target_pairs={{0,16},{8,24},{16,0},{24,8},{1,17},{9,25},{17,1},{25,9},{2,18},{10... | collective-permute-start | bytes 98312 | tf_op jit(solution)/shard_map/ppermute | solution.py:45
  14.5 0.1 collective-permute-start.5
  14.6 1.9 %collective-permute-start.4 = (bf16[128,1024]{1,0:T(8,128)(2,1)S(1)}, bf16[128,1024]{1,0:T(8,128)(2,1)S(1)}, u32[]{:S(2)}, u32[]{:S(2)}) collective-permute-start(bf16[128,1024]{1,0:T(8,128)(2,1)S(1)} %get-tuple-element.29.own_ref.far_ref), channel_id=1, source_target_pairs={{0,8},{1,2},{2,1},{3,4},{4,3},{5,6},{6,5},{7,15},{8,0},{9,10},{10,... | collective-permute-start | bytes 786440 | tf_op jit(solution)/shard_map/ppermute | solution.py:35
  16.5 1.2 %toeplitz.1 = (bf16[128,256,128]{2,1,0:T(8,128)(2,1)S(1)}, f32[8,128]{1,0:T(8,128)S(1)}) custom-call(bf16[128,128]{1,0:T(8,128)(2,1)S(1)} %copy-done.1, f32[64,128]{1,0:T(8,128)S(1)} %filter_gradient.1.after_ref.refs_0_), custom_call_target="tpu_custom_call" | custom-call | flops 134217728 | bytes 8388608 | tf_op jit(solution)/shard_map/toeplitz/pallas_call | solution.py:276
  17.8 0.1 collective-permute-done.6.refs_2_
  17.9 0.5 %collective-permute-done.5.refs_1_ = f32[64,128]{1,0:T(8,128)S(1)} collective-permute-done((f32[64,128]{1,0:T(8,128)S(1)}, f32[64,128]{1,0:T(8,128)S(1)}, u32[]{:S(2)}, u32[]{:S(2)}) %collective-permute-start.5) | collective-permute-done | bytes 32800 | tf_op jit(solution)/shard_map/ppermute | solution.py:45
  18.4 1.1 %collective-permute-start.8 = (f32[64,128]{1,0:T(8,128)S(1)}, f32[64,128]{1,0:T(8,128)S(1)}, u32[]{:S(2)}, u32[]{:S(2)}) collective-permute-start(f32[64,128]{1,0:T(8,128)S(1)} %add.3.rest_0_.refs_0_), channel_id=1, source_target_pairs={{0,2},{1,3},{2,0},{3,1},{4,6},{5,7},{6,4},{7,5},{8,10},{9,11},{10,... | collective-permute-start | bytes 98312 | tf_op jit(solution)/shard_map/ppermute | solution.py:45
  19.5 2.3 %outputs_0.1 = (bf16[128,2048]{1,0:T(8,128)(2,1)}, bf16[128,2048]{1,0:T(8,128)(2,1)}, bf16[128,2048]{1,0:T(8,128)(2,1)}, bf16[128,2048]{1,0:T(8,128)(2,1)}, f32[8,128]{1,0:T(8,128)S(1)}) custom-call(bf16[128,2048]{1,0:T(8,128)(2,1)S(1)} %get-tuple-element.24.q_ref, bf16[128,2048]{1,0:T(8,128)(2,1)S(1)} %get-tuple-element.25.k_ref, ...), custom_call_target="tpu_custom_call" | custom-call | flops 4294967296 | bytes 3145728 | tf_op jit(solution)/shard_map/outputs_0/pallas_call | solution.py:443
  21.8 0.6 %collective-permute-done.8.refs_1_ = f32[64,128]{1,0:T(8,128)S(1)} collective-permute-done((f32[64,128]{1,0:T(8,128)S(1)}, f32[64,128]{1,0:T(8,128)S(1)}, u32[]{:S(2)}, u32[]{:S(2)}) %collective-permute-start.8) | collective-permute-done | bytes 32800 | tf_op jit(solution)/shard_map/ppermute | solution.py:45
  22.4 2.5 %collective-permute-start.9 = (f32[64,128]{1,0:T(8,128)S(1)}, f32[64,128]{1,0:T(8,128)S(1)}, u32[]{:S(2)}, u32[]{:S(2)}) collective-permute-start(f32[64,128]{1,0:T(8,128)S(1)} %add.4.rest_0_.refs_0_), channel_id=1, source_target_pairs={{0,4},{1,5},{2,6},{3,7},{4,0},{5,1},{6,2},{7,3},{8,12},{9,13},{10,... | collective-permute-start | bytes 98312 | tf_op jit(solution)/shard_map/ppermute | solution.py:45
  24.9 2.3 %outputs_1.1 = (bf16[128,2048]{1,0:T(8,128)(2,1)}, bf16[128,2048]{1,0:T(8,128)(2,1)}, bf16[128,2048]{1,0:T(8,128)(2,1)}, bf16[128,2048]{1,0:T(8,128)(2,1)}, f32[8,128]{1,0:T(8,128)S(1)}) custom-call(bf16[128,2048]{1,0:T(8,128)(2,1)S(1)} %get-tuple-element.24.q_ref, ...), custom_call_target="tpu_custom_call", output_to_operand_aliasing={{0}: (11, {}), {1}: (12, {}), {2}: (13, {}), {3}: (14, {})} | custom-call | flops 4294967296 | bytes 3145728 | tf_op jit(solution)/shard_map/outputs_1/pallas_call | solution.py:443
  27.3 1.2 %collective-permute-done.10.other_ref = f32[64,128]{1,0:T(8,128)S(1)} collective-permute-done((f32[64,128]{1,0:T(8,128)S(1)}, f32[64,128]{1,0:T(8,128)S(1)}, u32[]{:S(2)}, u32[]{:S(2)}) %collective-permute-start.10) | collective-permute-done | bytes 32800 | tf_op jit(solution)/shard_map/ppermute | solution.py:35
  28.5 0.6 %join.1 = f32[128,128]{1,0:T(8,128)} custom-call(f32[64,128]{1,0:T(8,128)S(1)} %add.5.mine_ref, f32[64,128]{1,0:T(8,128)S(1)} %collective-permute-done.10.other_ref), custom_call_target="tpu_custom_call" | custom-call | tf_op jit(solution)/shard_map/join/pallas_call | solution.py:94
  (13 shorter events, 0.1 us)
Async XLA Ops:
  0.6 15.9 %copy-start.1 = (bf16[128,128]{1,0:T(8,128)(2,1)S(1)}, bf16[128,128]{1,0:T(8,128)(2,1)}, u32[]{:S(2)}) copy-start(bf16[128,128]{1,0:T(8,128)(2,1)} %filters_ref.1) | copy-start | bytes 98308
  2.0 7.4 %collective-permute-start.2 = (bf16[128,1024]{1,0:T(8,128)(2,1)S(1)}, bf16[128,1024]{1,0:T(8,128)(2,1)S(1)}, u32[]{:S(2)}, u32[]{:S(2)}) collective-permute-start(bf16[128,1024]{1,0:T(8,128)(2,1)S(1)} %first_gate.1.after_ref.far_ref), channel_id=1, source_target_pairs={{0,8},{1,2},{2,1},{3,4},{4,3},{5,6},{6,5},{7,15},{8,0},{9,10},{10,... | collective-permute-start | bytes 786440 | tf_op jit(solution)/shard_map/ppermute | solution.py:35
  5.0 4.4 %collective-permute-start.1 = (bf16[128,1024]{1,0:T(8,128)(2,1)S(1)}, bf16[128,1024]{1,0:T(8,128)(2,1)S(1)}, u32[]{:S(2)}, u32[]{:S(2)}) collective-permute-start(bf16[128,1024]{1,0:T(8,128)(2,1)S(1)} %first_gate.1.after_ref.far_ref), channel_id=1, source_target_pairs={{0,1},{1,0},{2,3},{3,2},{4,5},{5,4},{6,7},{7,6},{8,9},{9,8},{10,11... | collective-permute-start | bytes 786440 | tf_op jit(solution)/shard_map/ppermute | solution.py:35
  7.1 2.4 %collective-permute-start.3 = (bf16[128,1024]{1,0:T(8,128)(2,1)S(1)}, bf16[128,1024]{1,0:T(8,128)(2,1)S(1)}, u32[]{:S(2)}, u32[]{:S(2)}) collective-permute-start(bf16[128,1024]{1,0:T(8,128)(2,1)S(1)} %get-tuple-element.28.near_ref), channel_id=1, source_target_pairs={{0,1},{1,0},{2,3},{3,2},{4,5},{5,4},{6,7},{7,6},{8,9},{9,8},{10,11... | collective-permute-start | bytes 786440 | tf_op jit(solution)/shard_map/ppermute | solution.py:35
  7.7 1.7 %collective-permute-start = (bf16[128,1024]{1,0:T(8,128)(2,1)S(1)}, bf16[128,1024]{1,0:T(8,128)(2,1)S(1)}, u32[]{:S(2)}, u32[]{:S(2)}) collective-permute-start(bf16[128,1024]{1,0:T(8,128)(2,1)S(1)} %get-tuple-element.30.after_ref.near_ref), channel_id=1, source_target_pairs={{0,1},{1,0},{2,3},{3,2},{4,5},{5,4},{6,7},{7,6},{8,9},{9,8},{10,11... | collective-permute-start | bytes 786440 | tf_op jit(solution)/shard_map/ppermute | solution.py:35
  7.7 0.7 %copy-start = (s32[1,3]{1,0:T(1,128)S(1)}, s32[1,3]{1,0:T(1,128)}, u32[]{:S(2)}) copy-start(s32[1,3]{1,0:T(1,128)} %param.10) | copy-start | bytes 40
  11.0 6.8 %collective-permute-start.7 = (f32[64,128]{1,0:T(8,128)S(1)}, f32[64,128]{1,0:T(8,128)S(1)}, u32[]{:S(2)}, u32[]{:S(2)}) collective-permute-start(f32[64,128]{1,0:T(8,128)S(1)} %filter_gradient.1.after_ref.refs_0_), channel_id=1, source_target_pairs={{0,24},{8,16},{16,8},{24,0},{1,25},{9,17},{17,9},{25,1},{2,26},{10... | collective-permute-start | bytes 98312 | tf_op jit(solution)/shard_map/ppermute | solution.py:45
  14.0 3.9 %collective-permute-start.6 = (f32[64,128]{1,0:T(8,128)S(1)}, f32[64,128]{1,0:T(8,128)S(1)}, u32[]{:S(2)}, u32[]{:S(2)}) collective-permute-start(f32[64,128]{1,0:T(8,128)S(1)} %filter_gradient.1.after_ref.refs_0_), channel_id=1, source_target_pairs={{0,16},{8,24},{16,0},{24,8},{1,17},{9,25},{17,1},{25,9},{2,18},{10... | collective-permute-start | bytes 98312 | tf_op jit(solution)/shard_map/ppermute | solution.py:45
  14.5 3.9 %collective-permute-start.5 = (f32[64,128]{1,0:T(8,128)S(1)}, f32[64,128]{1,0:T(8,128)S(1)}, u32[]{:S(2)}, u32[]{:S(2)}) collective-permute-start(f32[64,128]{1,0:T(8,128)S(1)} %filter_gradient.1.after_ref.refs_0_), channel_id=1, source_target_pairs={{0,8},{8,0},{16,24},{24,16},{1,9},{9,1},{17,25},{25,17},{2,10},{10... | collective-permute-start | bytes 98312 | tf_op jit(solution)/shard_map/ppermute | solution.py:45
  14.6 10.3 %collective-permute-start.4 = (bf16[128,1024]{1,0:T(8,128)(2,1)S(1)}, bf16[128,1024]{1,0:T(8,128)(2,1)S(1)}, u32[]{:S(2)}, u32[]{:S(2)}) collective-permute-start(bf16[128,1024]{1,0:T(8,128)(2,1)S(1)} %get-tuple-element.29.own_ref.far_ref), channel_id=1, source_target_pairs={{0,8},{1,2},{2,1},{3,4},{4,3},{5,6},{6,5},{7,15},{8,0},{9,10},{10,... | collective-permute-start | bytes 786440 | tf_op jit(solution)/shard_map/ppermute | solution.py:35
  18.4 4.0 %collective-permute-start.8 = (f32[64,128]{1,0:T(8,128)S(1)}, f32[64,128]{1,0:T(8,128)S(1)}, u32[]{:S(2)}, u32[]{:S(2)}) collective-permute-start(f32[64,128]{1,0:T(8,128)S(1)} %add.3.rest_0_.refs_0_), channel_id=1, source_target_pairs={{0,2},{1,3},{2,0},{3,1},{4,6},{5,7},{6,4},{7,5},{8,10},{9,11},{10,... | collective-permute-start | bytes 98312 | tf_op jit(solution)/shard_map/ppermute | solution.py:45
  22.4 4.8 %collective-permute-start.9 = (f32[64,128]{1,0:T(8,128)S(1)}, f32[64,128]{1,0:T(8,128)S(1)}, u32[]{:S(2)}, u32[]{:S(2)}) collective-permute-start(f32[64,128]{1,0:T(8,128)S(1)} %add.4.rest_0_.refs_0_), channel_id=1, source_target_pairs={{0,4},{1,5},{2,6},{3,7},{4,0},{5,1},{6,2},{7,3},{8,12},{9,13},{10,... | collective-permute-start | bytes 98312 | tf_op jit(solution)/shard_map/ppermute | solution.py:45
  27.2 1.2 %collective-permute-start.10 = (f32[64,128]{1,0:T(8,128)S(1)}, f32[64,128]{1,0:T(8,128)S(1)}, u32[]{:S(2)}, u32[]{:S(2)}) collective-permute-start(f32[64,128]{1,0:T(8,128)S(1)} %add.5.mine_ref), channel_id=1, source_target_pairs={{0,1},{1,0},{2,3},{3,2},{4,5},{5,4},{6,7},{7,6},{8,9},{9,8},{10,11... | collective-permute-start | bytes 98312 | tf_op jit(solution)/shard_map/ppermute | solution.py:35
where the time goes:
time: 29.3 us; the launch traced here: 29.1 us
  starting transfers between devices  13 us (44%)
  Pallas kernels  11.8 us (40%)
  waiting for transfers between devices  2.95 us (10%)
  between operations  0.72 us (2%)
  local copies, waits for them, and re-layouts  0.66 us (2%)
    ppermute x5, starting transfers between devices, swapped(): return lax.ppermute(array, axis, [(i, i ^ step) for i in range(size)])  7.16 us
    ppermute x6, starting transfers between devices, exchange(): return lax.ppermute(array, ('dp', 'ctx'), pairs)  5.84 us
    pallas_call x2, Pallas kernels, outputs(): pl.pallas_call(functools.partial(outputs_kernel, width, piece * part), in...  4.57 us
    pallas_call x1, Pallas kernels, gates(): pl.pallas_call(gates_kernel, in_specs=[pl.BlockSpec(memory_space=pl.ANY)]...  1.8 us
    ppermute x6, waiting for transfers between devices, exchange(): return lax.ppermute(array, ('dp', 'ctx'), pairs)  1.64 us
    pallas_call x1, Pallas kernels, filter_gradient(): pl.pallas_call(functools.partial(filter_grad_kernel, width), in_specs=[VM...  1.6 us
    pallas_call x1, Pallas kernels, first_gate(): pl.pallas_call(first_kernel, in_specs=[pl.BlockSpec(memory_space=pltpu.HB...  1.39 us
    ppermute x5, waiting for transfers between devices, swapped(): return lax.ppermute(array, axis, [(i, i ^ step) for i in range(size)])  1.31 us
  transfers between devices with their start and end apart: 11, of which 6 were waited for; matrix products, arithmetic and copies ran while one was open for 0% of the time, Pallas kernels for 28%

commit v1 on v0

--- a/solution.py
+++ b/solution.py
@@ -8,7 +8,7 @@
 from jax.sharding import PartitionSpec as P
 
 LANES = 128
-ROW_BLOCK = 32
+ROW_BLOCK = 64
 MIB = 1024 * 1024
 CHUNKS = 4
 PIECES = 2

time: 29.3 us -> 29.3 us (level)
  no operation moved by 1% of the time
where the time goes in v1:
time: 29.3 us; the launch traced here: 29.1 us
  starting transfers between devices  13.1 us (45%)
  Pallas kernels  11.7 us (40%)
  waiting for transfers between devices  2.95 us (10%)
  between operations  0.73 us (2%)
  local copies, waits for them, and re-layouts  0.66 us (2%)
    ppermute x5, starting transfers between devices, swapped(): return lax.ppermute(array, axis, [(i, i ^ step) for i in range(size)])  7.23 us
    ppermute x6, starting transfers between devices, exchange(): return lax.ppermute(array, ('dp', 'ctx'), pairs)  5.82 us
    pallas_call x2, Pallas kernels, outputs(): pl.pallas_call(functools.partial(outputs_kernel, width, piece * part), in...  4.56 us
    pallas_call x1, Pallas kernels, gates(): pl.pallas_call(gates_kernel, in_specs=[pl.BlockSpec(memory_space=pl.ANY)]...  1.8 us
    ppermute x6, waiting for transfers between devices, exchange(): return lax.ppermute(array, ('dp', 'ctx'), pairs)  1.64 us
    pallas_call x1, Pallas kernels, filter_gradient(): pl.pallas_call(functools.partial(filter_grad_kernel, width), in_specs=[VM...  1.54 us
    pallas_call x1, Pallas kernels, first_gate(): pl.pallas_call(first_kernel, in_specs=[pl.BlockSpec(memory_space=pltpu.HB...  1.39 us
    ppermute x5, waiting for transfers between devices, swapped(): return lax.ppermute(array, axis, [(i, i ^ step) for i in range(size)])  1.31 us
  transfers between devices with their start and end apart: 11, of which 6 were waited for; matrix products, arithmetic and copies ran while one was open for 0% of the time, Pallas kernels for 28%

profile of v1, /device:TPU:0, one launch (start us, length us, event | category | flops | bytes accessed | tf_op | source)
XLA Modules:
  0.0 29.1 jit_solution(687226648758544733)
XLA Ops:
  0.6 1.4 %first_gate.1.after_ref.far_ref = bf16[128,1024]{1,0:T(8,128)(2,1)S(1)} custom-call(bf16[128,2048]{1,0:T(8,128)(2,1)} %bitcast.10, bf16[128,2048]{1,0:T(8,128)(2,1)} %bitcast.12, bf16[128,2048]{1,0:T(8,128)(2,1)} %bitcast.14, bf16[128,2048]{1,0:T(8,128)(2,1)} %bitcast.16), custom_call_target="tpu_custom_call" | custom-call | flops 33554432 | bytes 786432 | tf_op jit(solution)/shard_map/first_gate/pallas_call | solution.py:154
  2.0 3.0 %collective-permute-start.2 = (bf16[128,1024]{1,0:T(8,128)(2,1)S(1)}, bf16[128,1024]{1,0:T(8,128)(2,1)S(1)}, u32[]{:S(2)}, u32[]{:S(2)}) collective-permute-start(bf16[128,1024]{1,0:T(8,128)(2,1)S(1)} %first_gate.1.after_ref.far_ref), channel_id=1, source_target_pairs={{0,8},{1,2},{2,1},{3,4},{4,3},{5,6},{6,5},{7,15},{8,0},{9,10},{10,... | collective-permute-start | bytes 786440 | tf_op jit(solution)/shard_map/ppermute | solution.py:35
  5.0 0.2 collective-permute-start.1
  5.2 1.8 %gates.1 = (bf16[128,2048]{1,0:T(8,128)(2,1)S(1)}, bf16[128,2048]{1,0:T(8,128)(2,1)S(1)}, bf16[128,2048]{1,0:T(8,128)(2,1)S(1)}, bf16[128,2048]{1,0:T(8,128)(2,1...) custom-call(bf16[128,1024]{1,0:T(8,128)(2,1)S(1)} %first_gate.1.after_ref.far_ref, ...), custom_call_target="tpu_custom_call" | custom-call | flops 67108864 | bytes 3145728 | tf_op jit(solution)/shard_map/gates/pallas_call | solution.py:224
  7.1 0.6 %collective-permute-start.3 = (bf16[128,1024]{1,0:T(8,128)(2,1)S(1)}, bf16[128,1024]{1,0:T(8,128)(2,1)S(1)}, u32[]{:S(2)}, u32[]{:S(2)}) collective-permute-start(bf16[128,1024]{1,0:T(8,128)(2,1)S(1)} %get-tuple-element.28.near_ref), channel_id=1, source_target_pairs={{0,1},{1,0},{2,3},{3,2},{4,5},{5,4},{6,7},{7,6},{8,9},{9,8},{10,11... | collective-permute-start | bytes 786440 | tf_op jit(solution)/shard_map/ppermute | solution.py:35
  7.7 0.1 collective-permute-start
  7.7 0.7 %copy-done = s32[1,3]{1,0:T(1,128)S(1)} copy-done((s32[1,3]{1,0:T(1,128)S(1)}, s32[1,3]{1,0:T(1,128)}, u32[]{:S(2)}) %copy-start) | copy-done | bytes 36
  8.4 0.6 %masks.1.keep_ref = bf16[2,16,128]{2,1,0:T(8,128)(2,1)S(1)} custom-call(s32[3]{0:T(128)S(1)} %bitcast.9, bf16[128,1024]{1,0:T(8,128)(2,1)S(1)} %get-tuple-element.30.after_ref.near_ref), custom_call_target="tpu_custom_call" | custom-call | tf_op jit(solution)/shard_map/masks/pallas_call | solution.py:251
  9.0 0.4 %collective-permute-done.2.far_in_ref = bf16[128,1024]{1,0:T(8,128)(2,1)S(1)} collective-permute-done((bf16[128,1024]{1,0:T(8,128)(2,1)S(1)}, bf16[128,1024]{1,0:T(8,128)(2,1)S(1)}, u32[]{:S(2)}, u32[]{:S(2)}) %collective-permute-start.2) | collective-permute-done | bytes 262176 | tf_op jit(solution)/shard_map/ppermute | solution.py:35
  9.4 1.5 %filter_gradient.1.after_ref.refs_0_ = f32[64,128]{1,0:T(8,128)S(1)} custom-call(bf16[128,1024]{1,0:T(8,128)(2,1)S(1)} %get-tuple-element.28.near_ref, bf16[128,1024]{1,0:T(8,128)(2,1)S(1)} %get-tuple-element.29.own_ref.far_ref, bf16[2,16,128]{2,1,0:T(8,128)(2,1)S(1)} %masks.1.keep_ref, bf16[128,1024]{1,0:T(8,128)(2,1)S(1)} %collective-permute-done.near_in_ref, ...), custom_call_target="tpu_custom_call" | custom-call | flops 1073741824 | bytes 2097152 | tf_op jit(solution)/shard_map/filter_gradient/pallas_call | solution.py:347
  11.0 3.0 %collective-permute-start.7 = (f32[64,128]{1,0:T(8,128)S(1)}, f32[64,128]{1,0:T(8,128)S(1)}, u32[]{:S(2)}, u32[]{:S(2)}) collective-permute-start(f32[64,128]{1,0:T(8,128)S(1)} %filter_gradient.1.after_ref.refs_0_), channel_id=1, source_target_pairs={{0,24},{8,16},{16,8},{24,0},{1,25},{9,17},{17,9},{25,1},{2,26},{10... | collective-permute-start | bytes 98312 | tf_op jit(solution)/shard_map/ppermute | solution.py:45
  14.0 0.5 %collective-permute-start.6 = (f32[64,128]{1,0:T(8,128)S(1)}, f32[64,128]{1,0:T(8,128)S(1)}, u32[]{:S(2)}, u32[]{:S(2)}) collective-permute-start(f32[64,128]{1,0:T(8,128)S(1)} %filter_gradient.1.after_ref.refs_0_), channel_id=1, source_target_pairs={{0,16},{8,24},{16,0},{24,8},{1,17},{9,25},{17,1},{25,9},{2,18},{10... | collective-permute-start | bytes 98312 | tf_op jit(solution)/shard_map/ppermute | solution.py:45
  14.5 0.1 collective-permute-start.5
  14.6 1.9 %collective-permute-start.4 = (bf16[128,1024]{1,0:T(8,128)(2,1)S(1)}, bf16[128,1024]{1,0:T(8,128)(2,1)S(1)}, u32[]{:S(2)}, u32[]{:S(2)}) collective-permute-start(bf16[128,1024]{1,0:T(8,128)(2,1)S(1)} %get-tuple-element.29.own_ref.far_ref), channel_id=1, source_target_pairs={{0,8},{1,2},{2,1},{3,4},{4,3},{5,6},{6,5},{7,15},{8,0},{9,10},{10,... | collective-permute-start | bytes 786440 | tf_op jit(solution)/shard_map/ppermute | solution.py:35
  16.5 1.2 %toeplitz.1 = (bf16[128,256,128]{2,1,0:T(8,128)(2,1)S(1)}, f32[8,128]{1,0:T(8,128)S(1)}) custom-call(bf16[128,128]{1,0:T(8,128)(2,1)S(1)} %copy-done.1, f32[64,128]{1,0:T(8,128)S(1)} %filter_gradient.1.after_ref.refs_0_), custom_call_target="tpu_custom_call" | custom-call | flops 134217728 | bytes 8388608 | tf_op jit(solution)/shard_map/toeplitz/pallas_call | solution.py:276
  17.8 0.1 collective-permute-done.6.refs_2_
  17.9 0.5 %collective-permute-done.5.refs_1_ = f32[64,128]{1,0:T(8,128)S(1)} collective-permute-done((f32[64,128]{1,0:T(8,128)S(1)}, f32[64,128]{1,0:T(8,128)S(1)}, u32[]{:S(2)}, u32[]{:S(2)}) %collective-permute-start.5) | collective-permute-done | bytes 32800 | tf_op jit(solution)/shard_map/ppermute | solution.py:45
  18.4 1.1 %collective-permute-start.8 = (f32[64,128]{1,0:T(8,128)S(1)}, f32[64,128]{1,0:T(8,128)S(1)}, u32[]{:S(2)}, u32[]{:S(2)}) collective-permute-start(f32[64,128]{1,0:T(8,128)S(1)} %add.3.rest_0_.refs_0_), channel_id=1, source_target_pairs={{0,2},{1,3},{2,0},{3,1},{4,6},{5,7},{6,4},{7,5},{8,10},{9,11},{10,... | collective-permute-start | bytes 98312 | tf_op jit(solution)/shard_map/ppermute | solution.py:45
  19.5 2.3 %outputs_0.1 = (bf16[128,2048]{1,0:T(8,128)(2,1)}, bf16[128,2048]{1,0:T(8,128)(2,1)}, bf16[128,2048]{1,0:T(8,128)(2,1)}, bf16[128,2048]{1,0:T(8,128)(2,1)}, f32[8,128]{1,0:T(8,128)S(1)}) custom-call(bf16[128,2048]{1,0:T(8,128)(2,1)S(1)} %get-tuple-element.24.q_ref, bf16[128,2048]{1,0:T(8,128)(2,1)S(1)} %get-tuple-element.25.k_ref, ...), custom_call_target="tpu_custom_call" | custom-call | flops 4294967296 | bytes 3145728 | tf_op jit(solution)/shard_map/outputs_0/pallas_call | solution.py:443
  21.8 0.6 %collective-permute-done.8.refs_1_ = f32[64,128]{1,0:T(8,128)S(1)} collective-permute-done((f32[64,128]{1,0:T(8,128)S(1)}, f32[64,128]{1,0:T(8,128)S(1)}, u32[]{:S(2)}, u32[]{:S(2)}) %collective-permute-start.8) | collective-permute-done | bytes 32800 | tf_op jit(solution)/shard_map/ppermute | solution.py:45
  22.4 2.5 %collective-permute-start.9 = (f32[64,128]{1,0:T(8,128)S(1)}, f32[64,128]{1,0:T(8,128)S(1)}, u32[]{:S(2)}, u32[]{:S(2)}) collective-permute-start(f32[64,128]{1,0:T(8,128)S(1)} %add.4.rest_0_.refs_0_), channel_id=1, source_target_pairs={{0,4},{1,5},{2,6},{3,7},{4,0},{5,1},{6,2},{7,3},{8,12},{9,13},{10,... | collective-permute-start | bytes 98312 | tf_op jit(solution)/shard_map/ppermute | solution.py:45
  24.9 2.3 %outputs_1.1 = (bf16[128,2048]{1,0:T(8,128)(2,1)}, bf16[128,2048]{1,0:T(8,128)(2,1)}, bf16[128,2048]{1,0:T(8,128)(2,1)}, bf16[128,2048]{1,0:T(8,128)(2,1)}, f32[8,128]{1,0:T(8,128)S(1)}) custom-call(bf16[128,2048]{1,0:T(8,128)(2,1)S(1)} %get-tuple-element.24.q_ref, ...), custom_call_target="tpu_custom_call", output_to_operand_aliasing={{0}: (11, {}), {1}: (12, {}), {2}: (13, {}), {3}: (14, {})} | custom-call | flops 4294967296 | bytes 3145728 | tf_op jit(solution)/shard_map/outputs_1/pallas_call | solution.py:443
  27.3 1.2 %collective-permute-done.10.other_ref = f32[64,128]{1,0:T(8,128)S(1)} collective-permute-done((f32[64,128]{1,0:T(8,128)S(1)}, f32[64,128]{1,0:T(8,128)S(1)}, u32[]{:S(2)}, u32[]{:S(2)}) %collective-permute-start.10) | collective-permute-done | bytes 32800 | tf_op jit(solution)/shard_map/ppermute | solution.py:35
  28.5 0.6 %join.1 = f32[128,128]{1,0:T(8,128)} custom-call(f32[64,128]{1,0:T(8,128)S(1)} %add.5.mine_ref, f32[64,128]{1,0:T(8,128)S(1)} %collective-permute-done.10.other_ref), custom_call_target="tpu_custom_call" | custom-call | tf_op jit(solution)/shard_map/join/pallas_call | solution.py:94
  (13 shorter events, 0.1 us)
Async XLA Ops:
  0.6 15.9 %copy-start.1 = (bf16[128,128]{1,0:T(8,128)(2,1)S(1)}, bf16[128,128]{1,0:T(8,128)(2,1)}, u32[]{:S(2)}) copy-start(bf16[128,128]{1,0:T(8,128)(2,1)} %filters_ref.1) | copy-start | bytes 98308
  2.0 7.4 %collective-permute-start.2 = (bf16[128,1024]{1,0:T(8,128)(2,1)S(1)}, bf16[128,1024]{1,0:T(8,128)(2,1)S(1)}, u32[]{:S(2)}, u32[]{:S(2)}) collective-permute-start(bf16[128,1024]{1,0:T(8,128)(2,1)S(1)} %first_gate.1.after_ref.far_ref), channel_id=1, source_target_pairs={{0,8},{1,2},{2,1},{3,4},{4,3},{5,6},{6,5},{7,15},{8,0},{9,10},{10,... | collective-permute-start | bytes 786440 | tf_op jit(solution)/shard_map/ppermute | solution.py:35
  5.0 4.4 %collective-permute-start.1 = (bf16[128,1024]{1,0:T(8,128)(2,1)S(1)}, bf16[128,1024]{1,0:T(8,128)(2,1)S(1)}, u32[]{:S(2)}, u32[]{:S(2)}) collective-permute-start(bf16[128,1024]{1,0:T(8,128)(2,1)S(1)} %first_gate.1.after_ref.far_ref), channel_id=1, source_target_pairs={{0,1},{1,0},{2,3},{3,2},{4,5},{5,4},{6,7},{7,6},{8,9},{9,8},{10,11... | collective-permute-start | bytes 786440 | tf_op jit(solution)/shard_map/ppermute | solution.py:35
  7.1 2.4 %collective-permute-start.3 = (bf16[128,1024]{1,0:T(8,128)(2,1)S(1)}, bf16[128,1024]{1,0:T(8,128)(2,1)S(1)}, u32[]{:S(2)}, u32[]{:S(2)}) collective-permute-start(bf16[128,1024]{1,0:T(8,128)(2,1)S(1)} %get-tuple-element.28.near_ref), channel_id=1, source_target_pairs={{0,1},{1,0},{2,3},{3,2},{4,5},{5,4},{6,7},{7,6},{8,9},{9,8},{10,11... | collective-permute-start | bytes 786440 | tf_op jit(solution)/shard_map/ppermute | solution.py:35
  7.7 1.7 %collective-permute-start = (bf16[128,1024]{1,0:T(8,128)(2,1)S(1)}, bf16[128,1024]{1,0:T(8,128)(2,1)S(1)}, u32[]{:S(2)}, u32[]{:S(2)}) collective-permute-start(bf16[128,1024]{1,0:T(8,128)(2,1)S(1)} %get-tuple-element.30.after_ref.near_ref), channel_id=1, source_target_pairs={{0,1},{1,0},{2,3},{3,2},{4,5},{5,4},{6,7},{7,6},{8,9},{9,8},{10,11... | collective-permute-start | bytes 786440 | tf_op jit(solution)/shard_map/ppermute | solution.py:35
  7.7 0.7 %copy-start = (s32[1,3]{1,0:T(1,128)S(1)}, s32[1,3]{1,0:T(1,128)}, u32[]{:S(2)}) copy-start(s32[1,3]{1,0:T(1,128)} %param.10) | copy-start | bytes 40
  11.0 6.8 %collective-permute-start.7 = (f32[64,128]{1,0:T(8,128)S(1)}, f32[64,128]{1,0:T(8,128)S(1)}, u32[]{:S(2)}, u32[]{:S(2)}) collective-permute-start(f32[64,128]{1,0:T(8,128)S(1)} %filter_gradient.1.after_ref.refs_0_), channel_id=1, source_target_pairs={{0,24},{8,16},{16,8},{24,0},{1,25},{9,17},{17,9},{25,1},{2,26},{10... | collective-permute-start | bytes 98312 | tf_op jit(solution)/shard_map/ppermute | solution.py:45
  14.0 3.9 %collective-permute-start.6 = (f32[64,128]{1,0:T(8,128)S(1)}, f32[64,128]{1,0:T(8,128)S(1)}, u32[]{:S(2)}, u32[]{:S(2)}) collective-permute-start(f32[64,128]{1,0:T(8,128)S(1)} %filter_gradient.1.after_ref.refs_0_), channel_id=1, source_target_pairs={{0,16},{8,24},{16,0},{24,8},{1,17},{9,25},{17,1},{25,9},{2,18},{10... | collective-permute-start | bytes 98312 | tf_op jit(solution)/shard_map/ppermute | solution.py:45
  14.5 3.9 %collective-permute-start.5 = (f32[64,128]{1,0:T(8,128)S(1)}, f32[64,128]{1,0:T(8,128)S(1)}, u32[]{:S(2)}, u32[]{:S(2)}) collective-permute-start(f32[64,128]{1,0:T(8,128)S(1)} %filter_gradient.1.after_ref.refs_0_), channel_id=1, source_target_pairs={{0,8},{8,0},{16,24},{24,16},{1,9},{9,1},{17,25},{25,17},{2,10},{10... | collective-permute-start | bytes 98312 | tf_op jit(solution)/shard_map/ppermute | solution.py:45
  14.6 10.3 %collective-permute-start.4 = (bf16[128,1024]{1,0:T(8,128)(2,1)S(1)}, bf16[128,1024]{1,0:T(8,128)(2,1)S(1)}, u32[]{:S(2)}, u32[]{:S(2)}) collective-permute-start(bf16[128,1024]{1,0:T(8,128)(2,1)S(1)} %get-tuple-element.29.own_ref.far_ref), channel_id=1, source_target_pairs={{0,8},{1,2},{2,1},{3,4},{4,3},{5,6},{6,5},{7,15},{8,0},{9,10},{10,... | collective-permute-start | bytes 786440 | tf_op jit(solution)/shard_map/ppermute | solution.py:35
  18.4 4.0 %collective-permute-start.8 = (f32[64,128]{1,0:T(8,128)S(1)}, f32[64,128]{1,0:T(8,128)S(1)}, u32[]{:S(2)}, u32[]{:S(2)}) collective-permute-start(f32[64,128]{1,0:T(8,128)S(1)} %add.3.rest_0_.refs_0_), channel_id=1, source_target_pairs={{0,2},{1,3},{2,0},{3,1},{4,6},{5,7},{6,4},{7,5},{8,10},{9,11},{10,... | collective-permute-start | bytes 98312 | tf_op jit(solution)/shard_map/ppermute | solution.py:45
  22.4 4.8 %collective-permute-start.9 = (f32[64,128]{1,0:T(8,128)S(1)}, f32[64,128]{1,0:T(8,128)S(1)}, u32[]{:S(2)}, u32[]{:S(2)}) collective-permute-start(f32[64,128]{1,0:T(8,128)S(1)} %add.4.rest_0_.refs_0_), channel_id=1, source_target_pairs={{0,4},{1,5},{2,6},{3,7},{4,0},{5,1},{6,2},{7,3},{8,12},{9,13},{10,... | collective-permute-start | bytes 98312 | tf_op jit(solution)/shard_map/ppermute | solution.py:45
  27.2 1.2 %collective-permute-start.10 = (f32[64,128]{1,0:T(8,128)S(1)}, f32[64,128]{1,0:T(8,128)S(1)}, u32[]{:S(2)}, u32[]{:S(2)}) collective-permute-start(f32[64,128]{1,0:T(8,128)S(1)} %add.5.mine_ref), channel_id=1, source_target_pairs={{0,1},{1,0},{2,3},{3,2},{4,5},{5,4},{6,7},{7,6},{8,9},{9,8},{10,11... | collective-permute-start | bytes 98312 | tf_op jit(solution)/shard_map/ppermute | solution.py:35

commit v2 on v1

--- a/solution.py
+++ b/solution.py
@@ -12,7 +12,7 @@
 MIB = 1024 * 1024
 CHUNKS = 4
 PIECES = 2
-CHUNK = 512
+CHUNK = 1024
 FIRST_VMEM = 213 * MIB // 4
 GATES_VMEM = 101 * MIB // 2
 VMEM = pl.BlockSpec(memory_space=pltpu.VMEM)

time: 29.3 us -> 29.3 us (level)
  waiting for transfers between devices: 2.95 us -> 3.35 us
    ppermute x5, waiting for transfers between devices: 1.31 us -> 1.7 us  [swapped(): return lax.ppermute(array, axis, [(i, i ^ step) for i in range(size)])]
  transfers between devices with their start and end apart: 11 -> 11, of which waited for: 6 -> 6; matrix products, arithmetic and copies ran while one was open for 0% -> 0% of each run, Pallas kernels for 28% -> 27%
where the time goes in v2:
time: 29.3 us; the launch traced here: 29.1 us
  starting transfers between devices  12.9 us (44%)
  Pallas kernels  11.5 us (39%)
  waiting for transfers between devices  3.35 us (11%)
  between operations  0.73 us (2%)
  local copies, waits for them, and re-layouts  0.66 us (2%)
    ppermute x5, starting transfers between devices, swapped(): return lax.ppermute(array, axis, [(i, i ^ step) for i in range(size)])  7.1 us
    ppermute x6, starting transfers between devices, exchange(): return lax.ppermute(array, ('dp', 'ctx'), pairs)  5.78 us
    pallas_call x2, Pallas kernels, outputs(): pl.pallas_call(functools.partial(outputs_kernel, width, piece * part), in...  4.31 us
    pallas_call x1, Pallas kernels, gates(): pl.pallas_call(gates_kernel, in_specs=[pl.BlockSpec(memory_space=pl.ANY)]...  1.8 us
    ppermute x5, waiting for transfers between devices, swapped(): return lax.ppermute(array, axis, [(i, i ^ step) for i in range(size)])  1.7 us
    ppermute x6, waiting for transfers between devices, exchange(): return lax.ppermute(array, ('dp', 'ctx'), pairs)  1.64 us
    pallas_call x1, Pallas kernels, filter_gradient(): pl.pallas_call(functools.partial(filter_grad_kernel, width), in_specs=[VM...  1.54 us
    pallas_call x1, Pallas kernels, first_gate(): pl.pallas_call(first_kernel, in_specs=[pl.BlockSpec(memory_space=pltpu.HB...  1.39 us
  transfers between devices with their start and end apart: 11, of which 6 were waited for; matrix products, arithmetic and copies ran while one was open for 0% of the time, Pallas kernels for 27%

profile of v2, /device:TPU:0, one launch (start us, length us, event | category | flops | bytes accessed | tf_op | source)
XLA Modules:
  0.0 29.1 jit_solution(565466582284960662)
XLA Ops:
  0.6 1.4 %first_gate.1.after_ref.far_ref = bf16[128,1024]{1,0:T(8,128)(2,1)S(1)} custom-call(bf16[128,2048]{1,0:T(8,128)(2,1)} %bitcast.10, bf16[128,2048]{1,0:T(8,128)(2,1)} %bitcast.12, bf16[128,2048]{1,0:T(8,128)(2,1)} %bitcast.14, bf16[128,2048]{1,0:T(8,128)(2,1)} %bitcast.16), custom_call_target="tpu_custom_call" | custom-call | flops 33554432 | bytes 786432 | tf_op jit(solution)/shard_map/first_gate/pallas_call | solution.py:154
  2.0 3.0 %collective-permute-start.2 = (bf16[128,1024]{1,0:T(8,128)(2,1)S(1)}, bf16[128,1024]{1,0:T(8,128)(2,1)S(1)}, u32[]{:S(2)}, u32[]{:S(2)}) collective-permute-start(bf16[128,1024]{1,0:T(8,128)(2,1)S(1)} %first_gate.1.after_ref.far_ref), channel_id=1, source_target_pairs={{0,8},{1,2},{2,1},{3,4},{4,3},{5,6},{6,5},{7,15},{8,0},{9,10},{10,... | collective-permute-start | bytes 786440 | tf_op jit(solution)/shard_map/ppermute | solution.py:35
  5.0 0.2 collective-permute-start.1
  5.2 1.8 %gates.1 = (bf16[128,2048]{1,0:T(8,128)(2,1)S(1)}, bf16[128,2048]{1,0:T(8,128)(2,1)S(1)}, bf16[128,2048]{1,0:T(8,128)(2,1)S(1)}, bf16[128,2048]{1,0:T(8,128)(2,1...) custom-call(bf16[128,1024]{1,0:T(8,128)(2,1)S(1)} %first_gate.1.after_ref.far_ref, ...), custom_call_target="tpu_custom_call" | custom-call | flops 67108864 | bytes 3145728 | tf_op jit(solution)/shard_map/gates/pallas_call | solution.py:224
  7.1 0.6 %collective-permute-start.3 = (bf16[128,1024]{1,0:T(8,128)(2,1)S(1)}, bf16[128,1024]{1,0:T(8,128)(2,1)S(1)}, u32[]{:S(2)}, u32[]{:S(2)}) collective-permute-start(bf16[128,1024]{1,0:T(8,128)(2,1)S(1)} %get-tuple-element.28.near_ref), channel_id=1, source_target_pairs={{0,1},{1,0},{2,3},{3,2},{4,5},{5,4},{6,7},{7,6},{8,9},{9,8},{10,11... | collective-permute-start | bytes 786440 | tf_op jit(solution)/shard_map/ppermute | solution.py:35
  7.7 0.7 %copy-done = s32[1,3]{1,0:T(1,128)S(1)} copy-done((s32[1,3]{1,0:T(1,128)S(1)}, s32[1,3]{1,0:T(1,128)}, u32[]{:S(2)}) %copy-start) | copy-done | bytes 36
  8.4 0.6 %masks.1.keep_ref = bf16[2,16,128]{2,1,0:T(8,128)(2,1)S(1)} custom-call(s32[3]{0:T(128)S(1)} %bitcast.9, bf16[128,1024]{1,0:T(8,128)(2,1)S(1)} %get-tuple-element.30.after_ref.near_ref), custom_call_target="tpu_custom_call" | custom-call | tf_op jit(solution)/shard_map/masks/pallas_call | solution.py:251
  9.0 0.4 %collective-permute-done.2.far_in_ref = bf16[128,1024]{1,0:T(8,128)(2,1)S(1)} collective-permute-done((bf16[128,1024]{1,0:T(8,128)(2,1)S(1)}, bf16[128,1024]{1,0:T(8,128)(2,1)S(1)}, u32[]{:S(2)}, u32[]{:S(2)}) %collective-permute-start.2) | collective-permute-done | bytes 262176 | tf_op jit(solution)/shard_map/ppermute | solution.py:35
  9.4 1.5 %filter_gradient.1.after_ref.refs_0_ = f32[64,128]{1,0:T(8,128)S(1)} custom-call(bf16[128,1024]{1,0:T(8,128)(2,1)S(1)} %get-tuple-element.28.near_ref, bf16[128,1024]{1,0:T(8,128)(2,1)S(1)} %get-tuple-element.29.own_ref.far_ref, bf16[2,16,128]{2,1,0:T(8,128)(2,1)S(1)} %masks.1.keep_ref, bf16[128,1024]{1,0:T(8,128)(2,1)S(1)} %collective-permute-done.near_in_ref, ...), custom_call_target="tpu_custom_call" | custom-call | flops 1073741824 | bytes 2097152 | tf_op jit(solution)/shard_map/filter_gradient/pallas_call | solution.py:347
  11.0 3.0 %collective-permute-start.7 = (f32[64,128]{1,0:T(8,128)S(1)}, f32[64,128]{1,0:T(8,128)S(1)}, u32[]{:S(2)}, u32[]{:S(2)}) collective-permute-start(f32[64,128]{1,0:T(8,128)S(1)} %filter_gradient.1.after_ref.refs_0_), channel_id=1, source_target_pairs={{0,24},{8,16},{16,8},{24,0},{1,25},{9,17},{17,9},{25,1},{2,26},{10... | collective-permute-start | bytes 98312 | tf_op jit(solution)/shard_map/ppermute | solution.py:45
  14.0 0.5 %collective-permute-start.6 = (f32[64,128]{1,0:T(8,128)S(1)}, f32[64,128]{1,0:T(8,128)S(1)}, u32[]{:S(2)}, u32[]{:S(2)}) collective-permute-start(f32[64,128]{1,0:T(8,128)S(1)} %filter_gradient.1.after_ref.refs_0_), channel_id=1, source_target_pairs={{0,16},{8,24},{16,0},{24,8},{1,17},{9,25},{17,1},{25,9},{2,18},{10... | collective-permute-start | bytes 98312 | tf_op jit(solution)/shard_map/ppermute | solution.py:45
  14.5 0.1 collective-permute-start.5
  14.6 1.9 %collective-permute-start.4 = (bf16[128,1024]{1,0:T(8,128)(2,1)S(1)}, bf16[128,1024]{1,0:T(8,128)(2,1)S(1)}, u32[]{:S(2)}, u32[]{:S(2)}) collective-permute-start(bf16[128,1024]{1,0:T(8,128)(2,1)S(1)} %get-tuple-element.29.own_ref.far_ref), channel_id=1, source_target_pairs={{0,8},{1,2},{2,1},{3,4},{4,3},{5,6},{6,5},{7,15},{8,0},{9,10},{10,... | collective-permute-start | bytes 786440 | tf_op jit(solution)/shard_map/ppermute | solution.py:35
  16.5 1.2 %toeplitz.1 = (bf16[128,256,128]{2,1,0:T(8,128)(2,1)S(1)}, f32[8,128]{1,0:T(8,128)S(1)}) custom-call(bf16[128,128]{1,0:T(8,128)(2,1)S(1)} %copy-done.1, f32[64,128]{1,0:T(8,128)S(1)} %filter_gradient.1.after_ref.refs_0_), custom_call_target="tpu_custom_call" | custom-call | flops 134217728 | bytes 8388608 | tf_op jit(solution)/shard_map/toeplitz/pallas_call | solution.py:276
  17.8 0.1 collective-permute-done.6.refs_2_
  17.9 0.5 %collective-permute-done.5.refs_1_ = f32[64,128]{1,0:T(8,128)S(1)} collective-permute-done((f32[64,128]{1,0:T(8,128)S(1)}, f32[64,128]{1,0:T(8,128)S(1)}, u32[]{:S(2)}, u32[]{:S(2)}) %collective-permute-start.5) | collective-permute-done | bytes 32800 | tf_op jit(solution)/shard_map/ppermute | solution.py:45
  18.4 1.1 %collective-permute-start.8 = (f32[64,128]{1,0:T(8,128)S(1)}, f32[64,128]{1,0:T(8,128)S(1)}, u32[]{:S(2)}, u32[]{:S(2)}) collective-permute-start(f32[64,128]{1,0:T(8,128)S(1)} %add.3.rest_0_.refs_0_), channel_id=1, source_target_pairs={{0,2},{1,3},{2,0},{3,1},{4,6},{5,7},{6,4},{7,5},{8,10},{9,11},{10,... | collective-permute-start | bytes 98312 | tf_op jit(solution)/shard_map/ppermute | solution.py:45
  19.5 2.2 %outputs_0.1 = (bf16[128,2048]{1,0:T(8,128)(2,1)}, bf16[128,2048]{1,0:T(8,128)(2,1)}, bf16[128,2048]{1,0:T(8,128)(2,1)}, bf16[128,2048]{1,0:T(8,128)(2,1)}, f32[8,128]{1,0:T(8,128)S(1)}) custom-call(bf16[128,2048]{1,0:T(8,128)(2,1)S(1)} %get-tuple-element.24.q_ref, bf16[128,2048]{1,0:T(8,128)(2,1)S(1)} %get-tuple-element.25.k_ref, ...), custom_call_target="tpu_custom_call" | custom-call | flops 4294967296 | bytes 3145728 | tf_op jit(solution)/shard_map/outputs_0/pallas_call | solution.py:443
  21.7 0.7 %collective-permute-done.8.refs_1_ = f32[64,128]{1,0:T(8,128)S(1)} collective-permute-done((f32[64,128]{1,0:T(8,128)S(1)}, f32[64,128]{1,0:T(8,128)S(1)}, u32[]{:S(2)}, u32[]{:S(2)}) %collective-permute-start.8) | collective-permute-done | bytes 32800 | tf_op jit(solution)/shard_map/ppermute | solution.py:45
  22.4 2.3 %collective-permute-start.9 = (f32[64,128]{1,0:T(8,128)S(1)}, f32[64,128]{1,0:T(8,128)S(1)}, u32[]{:S(2)}, u32[]{:S(2)}) collective-permute-start(f32[64,128]{1,0:T(8,128)S(1)} %add.4.rest_0_.refs_0_), channel_id=1, source_target_pairs={{0,4},{1,5},{2,6},{3,7},{4,0},{5,1},{6,2},{7,3},{8,12},{9,13},{10,... | collective-permute-start | bytes 98312 | tf_op jit(solution)/shard_map/ppermute | solution.py:45
  24.8 2.2 %outputs_1.1 = (bf16[128,2048]{1,0:T(8,128)(2,1)}, bf16[128,2048]{1,0:T(8,128)(2,1)}, bf16[128,2048]{1,0:T(8,128)(2,1)}, bf16[128,2048]{1,0:T(8,128)(2,1)}, f32[8,128]{1,0:T(8,128)S(1)}) custom-call(bf16[128,2048]{1,0:T(8,128)(2,1)S(1)} %get-tuple-element.24.q_ref, ...), custom_call_target="tpu_custom_call", output_to_operand_aliasing={{0}: (11, {}), {1}: (12, {}), {2}: (13, {}), {3}: (14, {})} | custom-call | flops 4294967296 | bytes 3145728 | tf_op jit(solution)/shard_map/outputs_1/pallas_call | solution.py:443
  26.9 0.3 %collective-permute-done.9.refs_1_ = f32[64,128]{1,0:T(8,128)S(1)} collective-permute-done((f32[64,128]{1,0:T(8,128)S(1)}, f32[64,128]{1,0:T(8,128)S(1)}, u32[]{:S(2)}, u32[]{:S(2)}) %collective-permute-start.9) | collective-permute-done | bytes 32800 | tf_op jit(solution)/shard_map/ppermute | solution.py:45
  27.2 1.2 %collective-permute-done.10.other_ref = f32[64,128]{1,0:T(8,128)S(1)} collective-permute-done((f32[64,128]{1,0:T(8,128)S(1)}, f32[64,128]{1,0:T(8,128)S(1)}, u32[]{:S(2)}, u32[]{:S(2)}) %collective-permute-start.10) | collective-permute-done | bytes 32800 | tf_op jit(solution)/shard_map/ppermute | solution.py:35
  28.4 0.6 %join.1 = f32[128,128]{1,0:T(8,128)} custom-call(f32[64,128]{1,0:T(8,128)S(1)} %add.5.mine_ref, f32[64,128]{1,0:T(8,128)S(1)} %collective-permute-done.10.other_ref), custom_call_target="tpu_custom_call" | custom-call | tf_op jit(solution)/shard_map/join/pallas_call | solution.py:94
  (13 shorter events, 0.1 us)
Async XLA Ops:
  0.6 15.9 %copy-start.1 = (bf16[128,128]{1,0:T(8,128)(2,1)S(1)}, bf16[128,128]{1,0:T(8,128)(2,1)}, u32[]{:S(2)}) copy-start(bf16[128,128]{1,0:T(8,128)(2,1)} %filters_ref.1) | copy-start | bytes 98308
  2.0 7.4 %collective-permute-start.2 = (bf16[128,1024]{1,0:T(8,128)(2,1)S(1)}, bf16[128,1024]{1,0:T(8,128)(2,1)S(1)}, u32[]{:S(2)}, u32[]{:S(2)}) collective-permute-start(bf16[128,1024]{1,0:T(8,128)(2,1)S(1)} %first_gate.1.after_ref.far_ref), channel_id=1, source_target_pairs={{0,8},{1,2},{2,1},{3,4},{4,3},{5,6},{6,5},{7,15},{8,0},{9,10},{10,... | collective-permute-start | bytes 786440 | tf_op jit(solution)/shard_map/ppermute | solution.py:35
  5.0 4.4 %collective-permute-start.1 = (bf16[128,1024]{1,0:T(8,128)(2,1)S(1)}, bf16[128,1024]{1,0:T(8,128)(2,1)S(1)}, u32[]{:S(2)}, u32[]{:S(2)}) collective-permute-start(bf16[128,1024]{1,0:T(8,128)(2,1)S(1)} %first_gate.1.after_ref.far_ref), channel_id=1, source_target_pairs={{0,1},{1,0},{2,3},{3,2},{4,5},{5,4},{6,7},{7,6},{8,9},{9,8},{10,11... | collective-permute-start | bytes 786440 | tf_op jit(solution)/shard_map/ppermute | solution.py:35
  7.1 2.4 %collective-permute-start.3 = (bf16[128,1024]{1,0:T(8,128)(2,1)S(1)}, bf16[128,1024]{1,0:T(8,128)(2,1)S(1)}, u32[]{:S(2)}, u32[]{:S(2)}) collective-permute-start(bf16[128,1024]{1,0:T(8,128)(2,1)S(1)} %get-tuple-element.28.near_ref), channel_id=1, source_target_pairs={{0,1},{1,0},{2,3},{3,2},{4,5},{5,4},{6,7},{7,6},{8,9},{9,8},{10,11... | collective-permute-start | bytes 786440 | tf_op jit(solution)/shard_map/ppermute | solution.py:35
  7.7 1.7 %collective-permute-start = (bf16[128,1024]{1,0:T(8,128)(2,1)S(1)}, bf16[128,1024]{1,0:T(8,128)(2,1)S(1)}, u32[]{:S(2)}, u32[]{:S(2)}) collective-permute-start(bf16[128,1024]{1,0:T(8,128)(2,1)S(1)} %get-tuple-element.30.after_ref.near_ref), channel_id=1, source_target_pairs={{0,1},{1,0},{2,3},{3,2},{4,5},{5,4},{6,7},{7,6},{8,9},{9,8},{10,11... | collective-permute-start | bytes 786440 | tf_op jit(solution)/shard_map/ppermute | solution.py:35
  7.7 0.7 %copy-start = (s32[1,3]{1,0:T(1,128)S(1)}, s32[1,3]{1,0:T(1,128)}, u32[]{:S(2)}) copy-start(s32[1,3]{1,0:T(1,128)} %param.10) | copy-start | bytes 40
  11.0 6.8 %collective-permute-start.7 = (f32[64,128]{1,0:T(8,128)S(1)}, f32[64,128]{1,0:T(8,128)S(1)}, u32[]{:S(2)}, u32[]{:S(2)}) collective-permute-start(f32[64,128]{1,0:T(8,128)S(1)} %filter_gradient.1.after_ref.refs_0_), channel_id=1, source_target_pairs={{0,24},{8,16},{16,8},{24,0},{1,25},{9,17},{17,9},{25,1},{2,26},{10... | collective-permute-start | bytes 98312 | tf_op jit(solution)/shard_map/ppermute | solution.py:45
  14.0 3.9 %collective-permute-start.6 = (f32[64,128]{1,0:T(8,128)S(1)}, f32[64,128]{1,0:T(8,128)S(1)}, u32[]{:S(2)}, u32[]{:S(2)}) collective-permute-start(f32[64,128]{1,0:T(8,128)S(1)} %filter_gradient.1.after_ref.refs_0_), channel_id=1, source_target_pairs={{0,16},{8,24},{16,0},{24,8},{1,17},{9,25},{17,1},{25,9},{2,18},{10... | collective-permute-start | bytes 98312 | tf_op jit(solution)/shard_map/ppermute | solution.py:45
  14.5 3.9 %collective-permute-start.5 = (f32[64,128]{1,0:T(8,128)S(1)}, f32[64,128]{1,0:T(8,128)S(1)}, u32[]{:S(2)}, u32[]{:S(2)}) collective-permute-start(f32[64,128]{1,0:T(8,128)S(1)} %filter_gradient.1.after_ref.refs_0_), channel_id=1, source_target_pairs={{0,8},{8,0},{16,24},{24,16},{1,9},{9,1},{17,25},{25,17},{2,10},{10... | collective-permute-start | bytes 98312 | tf_op jit(solution)/shard_map/ppermute | solution.py:45
  14.6 10.1 %collective-permute-start.4 = (bf16[128,1024]{1,0:T(8,128)(2,1)S(1)}, bf16[128,1024]{1,0:T(8,128)(2,1)S(1)}, u32[]{:S(2)}, u32[]{:S(2)}) collective-permute-start(bf16[128,1024]{1,0:T(8,128)(2,1)S(1)} %get-tuple-element.29.own_ref.far_ref), channel_id=1, source_target_pairs={{0,8},{1,2},{2,1},{3,4},{4,3},{5,6},{6,5},{7,15},{8,0},{9,10},{10,... | collective-permute-start | bytes 786440 | tf_op jit(solution)/shard_map/ppermute | solution.py:35
  18.4 4.0 %collective-permute-start.8 = (f32[64,128]{1,0:T(8,128)S(1)}, f32[64,128]{1,0:T(8,128)S(1)}, u32[]{:S(2)}, u32[]{:S(2)}) collective-permute-start(f32[64,128]{1,0:T(8,128)S(1)} %add.3.rest_0_.refs_0_), channel_id=1, source_target_pairs={{0,2},{1,3},{2,0},{3,1},{4,6},{5,7},{6,4},{7,5},{8,10},{9,11},{10,... | collective-permute-start | bytes 98312 | tf_op jit(solution)/shard_map/ppermute | solution.py:45
  22.4 4.8 %collective-permute-start.9 = (f32[64,128]{1,0:T(8,128)S(1)}, f32[64,128]{1,0:T(8,128)S(1)}, u32[]{:S(2)}, u32[]{:S(2)}) collective-permute-start(f32[64,128]{1,0:T(8,128)S(1)} %add.4.rest_0_.refs_0_), channel_id=1, source_target_pairs={{0,4},{1,5},{2,6},{3,7},{4,0},{5,1},{6,2},{7,3},{8,12},{9,13},{10,... | collective-permute-start | bytes 98312 | tf_op jit(solution)/shard_map/ppermute | solution.py:45
  27.2 1.2 %collective-permute-start.10 = (f32[64,128]{1,0:T(8,128)S(1)}, f32[64,128]{1,0:T(8,128)S(1)}, u32[]{:S(2)}, u32[]{:S(2)}) collective-permute-start(f32[64,128]{1,0:T(8,128)S(1)} %add.5.mine_ref), channel_id=1, source_target_pairs={{0,1},{1,0},{2,3},{3,2},{4,5},{5,4},{6,7},{7,6},{8,9},{9,8},{10,11... | collective-permute-start | bytes 98312 | tf_op jit(solution)/shard_map/ppermute | solution.py:35

commit v3 on v2

--- a/solution.py
+++ b/solution.py
@@ -10,7 +10,7 @@
 LANES = 128
 ROW_BLOCK = 64
 MIB = 1024 * 1024
-CHUNKS = 4
+CHUNKS = 2
 PIECES = 2
 CHUNK = 1024
 FIRST_VMEM = 213 * MIB // 4

time: 29.3 us -> 29.2 us (level)
  no operation moved by 1% of the time
where the time goes in v3:
time: 29.2 us; the launch traced here: 29.1 us
  starting transfers between devices  12.8 us (44%)
  Pallas kernels  11.3 us (39%)
  waiting for transfers between devices  3.53 us (12%)
  between operations  0.73 us (2%)
  local copies, waits for them, and re-layouts  0.66 us (2%)
    ppermute x5, starting transfers between devices, swapped(): return lax.ppermute(array, axis, [(i, i ^ step) for i in range(size)])  7.09 us
    ppermute x6, starting transfers between devices, exchange(): return lax.ppermute(array, ('dp', 'ctx'), pairs)  5.72 us
    pallas_call x2, Pallas kernels, outputs(): pl.pallas_call(functools.partial(outputs_kernel, width, piece * part), in...  4.31 us
    ppermute x6, waiting for transfers between devices, exchange(): return lax.ppermute(array, ('dp', 'ctx'), pairs)  1.83 us
    ppermute x5, waiting for transfers between devices, swapped(): return lax.ppermute(array, axis, [(i, i ^ step) for i in range(size)])  1.7 us
    pallas_call x1, Pallas kernels, gates(): pl.pallas_call(gates_kernel, in_specs=[pl.BlockSpec(memory_space=pl.ANY)]...  1.68 us
    pallas_call x1, Pallas kernels, filter_gradient(): pl.pallas_call(functools.partial(filter_grad_kernel, width), in_specs=[VM...  1.54 us
    pallas_call x1, Pallas kernels, first_gate(): pl.pallas_call(first_kernel, in_specs=[pl.BlockSpec(memory_space=pltpu.HB...  1.38 us
  transfers between devices with their start and end apart: 11, of which 6 were waited for; matrix products, arithmetic and copies ran while one was open for 0% of the time, Pallas kernels for 27%

profile of v3, /device:TPU:0, one launch (start us, length us, event | category | flops | bytes accessed | tf_op | source)
XLA Modules:
  0.0 29.1 jit_solution(17211753043852817322)
XLA Ops:
  0.6 1.4 %first_gate.1.after_ref.far_ref = bf16[128,1024]{1,0:T(8,128)(2,1)S(1)} custom-call(bf16[128,2048]{1,0:T(8,128)(2,1)} %bitcast.10, bf16[128,2048]{1,0:T(8,128)(2,1)} %bitcast.12, bf16[128,2048]{1,0:T(8,128)(2,1)} %bitcast.14, bf16[128,2048]{1,0:T(8,128)(2,1)} %bitcast.16), custom_call_target="tpu_custom_call" | custom-call | flops 33554432 | bytes 786432 | tf_op jit(solution)/shard_map/first_gate/pallas_call | solution.py:154
  2.0 3.0 %collective-permute-start.2 = (bf16[128,1024]{1,0:T(8,128)(2,1)S(1)}, bf16[128,1024]{1,0:T(8,128)(2,1)S(1)}, u32[]{:S(2)}, u32[]{:S(2)}) collective-permute-start(bf16[128,1024]{1,0:T(8,128)(2,1)S(1)} %first_gate.1.after_ref.far_ref), channel_id=1, source_target_pairs={{0,8},{1,2},{2,1},{3,4},{4,3},{5,6},{6,5},{7,15},{8,0},{9,10},{10,... | collective-permute-start | bytes 786440 | tf_op jit(solution)/shard_map/ppermute | solution.py:35
  5.0 0.2 collective-permute-start.1
  5.2 1.7 %gates.1 = (bf16[128,2048]{1,0:T(8,128)(2,1)S(1)}, bf16[128,2048]{1,0:T(8,128)(2,1)S(1)}, bf16[128,2048]{1,0:T(8,128)(2,1)S(1)}, bf16[128,2048]{1,0:T(8,128)(2,1...) custom-call(bf16[128,1024]{1,0:T(8,128)(2,1)S(1)} %first_gate.1.after_ref.far_ref, ...), custom_call_target="tpu_custom_call" | custom-call | flops 67108864 | bytes 3145728 | tf_op jit(solution)/shard_map/gates/pallas_call | solution.py:224
  6.9 0.5 %collective-permute-start.3 = (bf16[128,1024]{1,0:T(8,128)(2,1)S(1)}, bf16[128,1024]{1,0:T(8,128)(2,1)S(1)}, u32[]{:S(2)}, u32[]{:S(2)}) collective-permute-start(bf16[128,1024]{1,0:T(8,128)(2,1)S(1)} %get-tuple-element.28.near_ref), channel_id=1, source_target_pairs={{0,1},{1,0},{2,3},{3,2},{4,5},{5,4},{6,7},{7,6},{8,9},{9,8},{10,11... | collective-permute-start | bytes 786440 | tf_op jit(solution)/shard_map/ppermute | solution.py:35
  7.5 0.7 %copy-done = s32[1,3]{1,0:T(1,128)S(1)} copy-done((s32[1,3]{1,0:T(1,128)S(1)}, s32[1,3]{1,0:T(1,128)}, u32[]{:S(2)}) %copy-start) | copy-done | bytes 36
  8.2 0.6 %masks.1.keep_ref = bf16[2,16,128]{2,1,0:T(8,128)(2,1)S(1)} custom-call(s32[3]{0:T(128)S(1)} %bitcast.9, bf16[128,1024]{1,0:T(8,128)(2,1)S(1)} %get-tuple-element.30.after_ref.near_ref), custom_call_target="tpu_custom_call" | custom-call | tf_op jit(solution)/shard_map/masks/pallas_call | solution.py:251
  8.8 0.6 %collective-permute-done.2.far_in_ref = bf16[128,1024]{1,0:T(8,128)(2,1)S(1)} collective-permute-done((bf16[128,1024]{1,0:T(8,128)(2,1)S(1)}, bf16[128,1024]{1,0:T(8,128)(2,1)S(1)}, u32[]{:S(2)}, u32[]{:S(2)}) %collective-permute-start.2) | collective-permute-done | bytes 262176 | tf_op jit(solution)/shard_map/ppermute | solution.py:35
  9.4 1.5 %filter_gradient.1.after_ref.refs_0_ = f32[64,128]{1,0:T(8,128)S(1)} custom-call(bf16[128,1024]{1,0:T(8,128)(2,1)S(1)} %get-tuple-element.28.near_ref, bf16[128,1024]{1,0:T(8,128)(2,1)S(1)} %get-tuple-element.29.own_ref.far_ref, bf16[2,16,128]{2,1,0:T(8,128)(2,1)S(1)} %masks.1.keep_ref, bf16[128,1024]{1,0:T(8,128)(2,1)S(1)} %collective-permute-done.near_in_ref, ...), custom_call_target="tpu_custom_call" | custom-call | flops 1073741824 | bytes 2097152 | tf_op jit(solution)/shard_map/filter_gradient/pallas_call | solution.py:347
  10.9 3.0 %collective-permute-start.7 = (f32[64,128]{1,0:T(8,128)S(1)}, f32[64,128]{1,0:T(8,128)S(1)}, u32[]{:S(2)}, u32[]{:S(2)}) collective-permute-start(f32[64,128]{1,0:T(8,128)S(1)} %filter_gradient.1.after_ref.refs_0_), channel_id=1, source_target_pairs={{0,24},{8,16},{16,8},{24,0},{1,25},{9,17},{17,9},{25,1},{2,26},{10... | collective-permute-start | bytes 98312 | tf_op jit(solution)/shard_map/ppermute | solution.py:45
  14.0 0.5 %collective-permute-start.6 = (f32[64,128]{1,0:T(8,128)S(1)}, f32[64,128]{1,0:T(8,128)S(1)}, u32[]{:S(2)}, u32[]{:S(2)}) collective-permute-start(f32[64,128]{1,0:T(8,128)S(1)} %filter_gradient.1.after_ref.refs_0_), channel_id=1, source_target_pairs={{0,16},{8,24},{16,0},{24,8},{1,17},{9,25},{17,1},{25,9},{2,18},{10... | collective-permute-start | bytes 98312 | tf_op jit(solution)/shard_map/ppermute | solution.py:45
  14.5 0.1 collective-permute-start.5
  14.6 1.9 %collective-permute-start.4 = (bf16[128,1024]{1,0:T(8,128)(2,1)S(1)}, bf16[128,1024]{1,0:T(8,128)(2,1)S(1)}, u32[]{:S(2)}, u32[]{:S(2)}) collective-permute-start(bf16[128,1024]{1,0:T(8,128)(2,1)S(1)} %get-tuple-element.29.own_ref.far_ref), channel_id=1, source_target_pairs={{0,8},{1,2},{2,1},{3,4},{4,3},{5,6},{6,5},{7,15},{8,0},{9,10},{10,... | collective-permute-start | bytes 786440 | tf_op jit(solution)/shard_map/ppermute | solution.py:35
  16.5 1.2 %toeplitz.1 = (bf16[128,256,128]{2,1,0:T(8,128)(2,1)S(1)}, f32[8,128]{1,0:T(8,128)S(1)}) custom-call(bf16[128,128]{1,0:T(8,128)(2,1)S(1)} %copy-done.1, f32[64,128]{1,0:T(8,128)S(1)} %filter_gradient.1.after_ref.refs_0_), custom_call_target="tpu_custom_call" | custom-call | flops 134217728 | bytes 8388608 | tf_op jit(solution)/shard_map/toeplitz/pallas_call | solution.py:276
  17.8 0.1 collective-permute-done.6.refs_2_
  17.9 0.5 %collective-permute-done.5.refs_1_ = f32[64,128]{1,0:T(8,128)S(1)} collective-permute-done((f32[64,128]{1,0:T(8,128)S(1)}, f32[64,128]{1,0:T(8,128)S(1)}, u32[]{:S(2)}, u32[]{:S(2)}) %collective-permute-start.5) | collective-permute-done | bytes 32800 | tf_op jit(solution)/shard_map/ppermute | solution.py:45
  18.4 1.1 %collective-permute-start.8 = (f32[64,128]{1,0:T(8,128)S(1)}, f32[64,128]{1,0:T(8,128)S(1)}, u32[]{:S(2)}, u32[]{:S(2)}) collective-permute-start(f32[64,128]{1,0:T(8,128)S(1)} %add.3.rest_0_.refs_0_), channel_id=1, source_target_pairs={{0,2},{1,3},{2,0},{3,1},{4,6},{5,7},{6,4},{7,5},{8,10},{9,11},{10,... | collective-permute-start | bytes 98312 | tf_op jit(solution)/shard_map/ppermute | solution.py:45
  19.5 2.2 %outputs_0.1 = (bf16[128,2048]{1,0:T(8,128)(2,1)}, bf16[128,2048]{1,0:T(8,128)(2,1)}, bf16[128,2048]{1,0:T(8,128)(2,1)}, bf16[128,2048]{1,0:T(8,128)(2,1)}, f32[8,128]{1,0:T(8,128)S(1)}) custom-call(bf16[128,2048]{1,0:T(8,128)(2,1)S(1)} %get-tuple-element.24.q_ref, bf16[128,2048]{1,0:T(8,128)(2,1)S(1)} %get-tuple-element.25.k_ref, ...), custom_call_target="tpu_custom_call" | custom-call | flops 4294967296 | bytes 3145728 | tf_op jit(solution)/shard_map/outputs_0/pallas_call | solution.py:443
  21.7 0.7 %collective-permute-done.8.refs_1_ = f32[64,128]{1,0:T(8,128)S(1)} collective-permute-done((f32[64,128]{1,0:T(8,128)S(1)}, f32[64,128]{1,0:T(8,128)S(1)}, u32[]{:S(2)}, u32[]{:S(2)}) %collective-permute-start.8) | collective-permute-done | bytes 32800 | tf_op jit(solution)/shard_map/ppermute | solution.py:45
  22.4 2.3 %collective-permute-start.9 = (f32[64,128]{1,0:T(8,128)S(1)}, f32[64,128]{1,0:T(8,128)S(1)}, u32[]{:S(2)}, u32[]{:S(2)}) collective-permute-start(f32[64,128]{1,0:T(8,128)S(1)} %add.4.rest_0_.refs_0_), channel_id=1, source_target_pairs={{0,4},{1,5},{2,6},{3,7},{4,0},{5,1},{6,2},{7,3},{8,12},{9,13},{10,... | collective-permute-start | bytes 98312 | tf_op jit(solution)/shard_map/ppermute | solution.py:45
  24.8 2.2 %outputs_1.1 = (bf16[128,2048]{1,0:T(8,128)(2,1)}, bf16[128,2048]{1,0:T(8,128)(2,1)}, bf16[128,2048]{1,0:T(8,128)(2,1)}, bf16[128,2048]{1,0:T(8,128)(2,1)}, f32[8,128]{1,0:T(8,128)S(1)}) custom-call(bf16[128,2048]{1,0:T(8,128)(2,1)S(1)} %get-tuple-element.24.q_ref, ...), custom_call_target="tpu_custom_call", output_to_operand_aliasing={{0}: (11, {}), {1}: (12, {}), {2}: (13, {}), {3}: (14, {})} | custom-call | flops 4294967296 | bytes 3145728 | tf_op jit(solution)/shard_map/outputs_1/pallas_call | solution.py:443
  26.9 0.3 %collective-permute-done.9.refs_1_ = f32[64,128]{1,0:T(8,128)S(1)} collective-permute-done((f32[64,128]{1,0:T(8,128)S(1)}, f32[64,128]{1,0:T(8,128)S(1)}, u32[]{:S(2)}, u32[]{:S(2)}) %collective-permute-start.9) | collective-permute-done | bytes 32800 | tf_op jit(solution)/shard_map/ppermute | solution.py:45
  27.2 1.2 %collective-permute-done.10.other_ref = f32[64,128]{1,0:T(8,128)S(1)} collective-permute-done((f32[64,128]{1,0:T(8,128)S(1)}, f32[64,128]{1,0:T(8,128)S(1)}, u32[]{:S(2)}, u32[]{:S(2)}) %collective-permute-start.10) | collective-permute-done | bytes 32800 | tf_op jit(solution)/shard_map/ppermute | solution.py:35
  28.4 0.6 %join.1 = f32[128,128]{1,0:T(8,128)} custom-call(f32[64,128]{1,0:T(8,128)S(1)} %add.5.mine_ref, f32[64,128]{1,0:T(8,128)S(1)} %collective-permute-done.10.other_ref), custom_call_target="tpu_custom_call" | custom-call | tf_op jit(solution)/shard_map/join/pallas_call | solution.py:94
  (13 shorter events, 0.1 us)
Async XLA Ops:
  0.6 15.9 %copy-start.1 = (bf16[128,128]{1,0:T(8,128)(2,1)S(1)}, bf16[128,128]{1,0:T(8,128)(2,1)}, u32[]{:S(2)}) copy-start(bf16[128,128]{1,0:T(8,128)(2,1)} %filters_ref.1) | copy-start | bytes 98308
  2.0 7.4 %collective-permute-start.2 = (bf16[128,1024]{1,0:T(8,128)(2,1)S(1)}, bf16[128,1024]{1,0:T(8,128)(2,1)S(1)}, u32[]{:S(2)}, u32[]{:S(2)}) collective-permute-start(bf16[128,1024]{1,0:T(8,128)(2,1)S(1)} %first_gate.1.after_ref.far_ref), channel_id=1, source_target_pairs={{0,8},{1,2},{2,1},{3,4},{4,3},{5,6},{6,5},{7,15},{8,0},{9,10},{10,... | collective-permute-start | bytes 786440 | tf_op jit(solution)/shard_map/ppermute | solution.py:35
  5.0 4.4 %collective-permute-start.1 = (bf16[128,1024]{1,0:T(8,128)(2,1)S(1)}, bf16[128,1024]{1,0:T(8,128)(2,1)S(1)}, u32[]{:S(2)}, u32[]{:S(2)}) collective-permute-start(bf16[128,1024]{1,0:T(8,128)(2,1)S(1)} %first_gate.1.after_ref.far_ref), channel_id=1, source_target_pairs={{0,1},{1,0},{2,3},{3,2},{4,5},{5,4},{6,7},{7,6},{8,9},{9,8},{10,11... | collective-permute-start | bytes 786440 | tf_op jit(solution)/shard_map/ppermute | solution.py:35
  6.9 2.5 %collective-permute-start.3 = (bf16[128,1024]{1,0:T(8,128)(2,1)S(1)}, bf16[128,1024]{1,0:T(8,128)(2,1)S(1)}, u32[]{:S(2)}, u32[]{:S(2)}) collective-permute-start(bf16[128,1024]{1,0:T(8,128)(2,1)S(1)} %get-tuple-element.28.near_ref), channel_id=1, source_target_pairs={{0,1},{1,0},{2,3},{3,2},{4,5},{5,4},{6,7},{7,6},{8,9},{9,8},{10,11... | collective-permute-start | bytes 786440 | tf_op jit(solution)/shard_map/ppermute | solution.py:35
  7.5 1.9 %collective-permute-start = (bf16[128,1024]{1,0:T(8,128)(2,1)S(1)}, bf16[128,1024]{1,0:T(8,128)(2,1)S(1)}, u32[]{:S(2)}, u32[]{:S(2)}) collective-permute-start(bf16[128,1024]{1,0:T(8,128)(2,1)S(1)} %get-tuple-element.30.after_ref.near_ref), channel_id=1, source_target_pairs={{0,1},{1,0},{2,3},{3,2},{4,5},{5,4},{6,7},{7,6},{8,9},{9,8},{10,11... | collective-permute-start | bytes 786440 | tf_op jit(solution)/shard_map/ppermute | solution.py:35
  7.5 0.7 %copy-start = (s32[1,3]{1,0:T(1,128)S(1)}, s32[1,3]{1,0:T(1,128)}, u32[]{:S(2)}) copy-start(s32[1,3]{1,0:T(1,128)} %param.10) | copy-start | bytes 40
  10.9 6.8 %collective-permute-start.7 = (f32[64,128]{1,0:T(8,128)S(1)}, f32[64,128]{1,0:T(8,128)S(1)}, u32[]{:S(2)}, u32[]{:S(2)}) collective-permute-start(f32[64,128]{1,0:T(8,128)S(1)} %filter_gradient.1.after_ref.refs_0_), channel_id=1, source_target_pairs={{0,24},{8,16},{16,8},{24,0},{1,25},{9,17},{17,9},{25,1},{2,26},{10... | collective-permute-start | bytes 98312 | tf_op jit(solution)/shard_map/ppermute | solution.py:45
  14.0 3.9 %collective-permute-start.6 = (f32[64,128]{1,0:T(8,128)S(1)}, f32[64,128]{1,0:T(8,128)S(1)}, u32[]{:S(2)}, u32[]{:S(2)}) collective-permute-start(f32[64,128]{1,0:T(8,128)S(1)} %filter_gradient.1.after_ref.refs_0_), channel_id=1, source_target_pairs={{0,16},{8,24},{16,0},{24,8},{1,17},{9,25},{17,1},{25,9},{2,18},{10... | collective-permute-start | bytes 98312 | tf_op jit(solution)/shard_map/ppermute | solution.py:45
  14.5 3.9 %collective-permute-start.5 = (f32[64,128]{1,0:T(8,128)S(1)}, f32[64,128]{1,0:T(8,128)S(1)}, u32[]{:S(2)}, u32[]{:S(2)}) collective-permute-start(f32[64,128]{1,0:T(8,128)S(1)} %filter_gradient.1.after_ref.refs_0_), channel_id=1, source_target_pairs={{0,8},{8,0},{16,24},{24,16},{1,9},{9,1},{17,25},{25,17},{2,10},{10... | collective-permute-start | bytes 98312 | tf_op jit(solution)/shard_map/ppermute | solution.py:45
  14.6 10.1 %collective-permute-start.4 = (bf16[128,1024]{1,0:T(8,128)(2,1)S(1)}, bf16[128,1024]{1,0:T(8,128)(2,1)S(1)}, u32[]{:S(2)}, u32[]{:S(2)}) collective-permute-start(bf16[128,1024]{1,0:T(8,128)(2,1)S(1)} %get-tuple-element.29.own_ref.far_ref), channel_id=1, source_target_pairs={{0,8},{1,2},{2,1},{3,4},{4,3},{5,6},{6,5},{7,15},{8,0},{9,10},{10,... | collective-permute-start | bytes 786440 | tf_op jit(solution)/shard_map/ppermute | solution.py:35
  18.4 4.0 %collective-permute-start.8 = (f32[64,128]{1,0:T(8,128)S(1)}, f32[64,128]{1,0:T(8,128)S(1)}, u32[]{:S(2)}, u32[]{:S(2)}) collective-permute-start(f32[64,128]{1,0:T(8,128)S(1)} %add.3.rest_0_.refs_0_), channel_id=1, source_target_pairs={{0,2},{1,3},{2,0},{3,1},{4,6},{5,7},{6,4},{7,5},{8,10},{9,11},{10,... | collective-permute-start | bytes 98312 | tf_op jit(solution)/shard_map/ppermute | solution.py:45
  22.4 4.8 %collective-permute-start.9 = (f32[64,128]{1,0:T(8,128)S(1)}, f32[64,128]{1,0:T(8,128)S(1)}, u32[]{:S(2)}, u32[]{:S(2)}) collective-permute-start(f32[64,128]{1,0:T(8,128)S(1)} %add.4.rest_0_.refs_0_), channel_id=1, source_target_pairs={{0,4},{1,5},{2,6},{3,7},{4,0},{5,1},{6,2},{7,3},{8,12},{9,13},{10,... | collective-permute-start | bytes 98312 | tf_op jit(solution)/shard_map/ppermute | solution.py:45
  27.2 1.2 %collective-permute-start.10 = (f32[64,128]{1,0:T(8,128)S(1)}, f32[64,128]{1,0:T(8,128)S(1)}, u32[]{:S(2)}, u32[]{:S(2)}) collective-permute-start(f32[64,128]{1,0:T(8,128)S(1)} %add.5.mine_ref), channel_id=1, source_target_pairs={{0,1},{1,0},{2,3},{3,2},{4,5},{5,4},{6,7},{7,6},{8,9},{9,8},{10,11... | collective-permute-start | bytes 98312 | tf_op jit(solution)/shard_map/ppermute | solution.py:35
